TPU v7x, 32 devices: a whole 2x2x4 slice. The times are simulated.
32 devices in a mesh: section: 2 (over y), ctx: 8 (over z, core), tp: 2 (over x).
Axes of the slice: x: 2, y: 2, z: 4, core: 2. Of those that a mesh axis runs over, the one named last changes fastest.
Arguments:
- x_in: bfloat16 [2, 2048, 2688], P(None, ('ctx', 'tp')), may hold values from -180 to 180
- norm_gain: bfloat16 [2, 2688], P('section'), may hold values from 0.099609375 to 1.8984375
- w_query: bfloat16 [2, 2688, 2048], P('section', None, 'tp'), may hold values from -1 to 1
- w_key: bfloat16 [2, 2688, 1024], P('section', 'ctx', 'tp'), may hold values from -3 to 3
- value_projection: bfloat16 [2, 2688, 1024], P('section', 'ctx', 'tp'), may hold values from -0.125 to 0.125
- w_out: bfloat16 [2, 2048, 2688], P('section', 'tp', 'ctx'), may hold values from -0.125 to 0.125
- doc_ids: int32 [2, 16], replicated, may hold values from 0 to 3, never falling along the last dimension, each value on 1 to 6 neighbouring positions
Outputs:
- layer_out: bfloat16 [2, 2, 2048, 2688], P('section', None, ('ctx', 'tp'))
Inputs may be any that keep to these rules, and one draw needn't show every extreme that they name: Along each row doc_ids never falls, so each document covers whole consecutive blocks of 128 tokens.
All inputs are finite; a program needn't handle non-finite values.
Results may differ from a plain program's by a relative error of at most 0.018.
Values may be sent and summed in bfloat16 or wider, within the bound.
No kernel may reach another device: no remote copies, remote signals or barrier semaphores. Data moves between devices by JAX's collectives and lax.ppermute only.
A program may use at most 128 MiB of HBM per device.

v0:
```python
import jax
import jax.numpy as jnp
from jax import lax
from jax.sharding import PartitionSpec as P

HEAD_SIZE = 128
WINDOW = 1024
BLOCK = 128


query_scale = 168.0 ** (-0.5)
rope_base = 10000.0


def shifted(shard, axis, by):
    count = lax.axis_size(axis)
    pairs = [(i, i + by) for i in range(count) if 0 <= i + by < count]
    return lax.ppermute(shard, axis, pairs)


def rms_normed(hidden, gain_row):
    widened = hidden.astype(jnp.float32)
    mean_square = jnp.mean(widened * widened, axis=-1, keepdims=True)
    return (widened * lax.rsqrt(mean_square + 1e-06) * gain_row.astype(jnp.float32)).astype(
        jnp.bfloat16
    )


def rotary_apply(tensor, token_position):
    half_dim = tensor.shape[-1] // 2
    frequency = rope_base ** (-(jnp.arange(half_dim, dtype=jnp.float32) * 2.0) / tensor.shape[-1])
    angles = token_position.astype(jnp.float32)[:, None] * frequency[None, :]
    cosine_table = jnp.cos(angles)[:, None, :]
    sine_table = jnp.sin(angles)[:, None, :]
    first_half = tensor[..., :half_dim]
    second_half = tensor[..., half_dim:]
    return jnp.concatenate(
        [
            first_half * cosine_table - second_half * sine_table,
            second_half * cosine_table + first_half * sine_table,
        ],
        axis=-1,
    )


def doc_lookup(ids_row, token_index, block):
    block_count = ids_row.shape[0]
    start_block = jnp.sum((ids_row[None, :] < ids_row[:, None]).astype(jnp.int32), axis=1)
    block_of = jnp.clip(token_index // block, 0, block_count - 1)
    onehot = (block_of[:, None] == jnp.arange(block_count, dtype=jnp.int32)[None, :]).astype(
        jnp.int32
    )
    start_of = jnp.sum(onehot * start_block[None, :], axis=1)
    doc_of = jnp.sum(onehot * ids_row[None, :], axis=1)
    return (token_index - start_of * block, doc_of)


def attention_rows(
    grouped_heads, key_matrix_rows, value_rows, query_index, query_doc, key_index, key_doc
):
    scores = (
        jnp.einsum(
            "qgrd,kgd->grqk", grouped_heads, key_matrix_rows, preferred_element_type=jnp.float32
        )
        * query_scale
    )
    allowed = (key_index[None, :] >= 0) & (key_index[None, :] <= query_index[:, None])
    allowed = (
        allowed
        & (query_index[:, None] - key_index[None, :] < WINDOW)
        & (key_doc[None, :] == query_doc[:, None])
    )
    scores = jnp.where(allowed[None, None], scores, -1e30)
    peak_score = jnp.max(scores, axis=-1, keepdims=True)
    raised = jnp.exp(scores - peak_score)
    weights = (raised / jnp.sum(raised, axis=-1, keepdims=True)).astype(jnp.bfloat16)
    layer_result = jnp.einsum(
        "grqk,kgd->qgrd", weights, value_rows, preferred_element_type=jnp.float32
    )
    return layer_result.astype(jnp.bfloat16).reshape(grouped_heads.shape[0], -1)


def local(x_in, norm_gain, w_query, w_key, value_projection, w_out, doc_ids):
    section_num = lax.axis_index("section")
    section_count = lax.axis_size("section")
    ctx_num = lax.axis_index("ctx")
    ctx_count = lax.axis_size("ctx")
    tp_count = lax.axis_size("tp")
    micro_count, half_rows, model_width = x_in.shape
    key_full, value_full, out_part = (
        lax.all_gather(w_key, "ctx", axis=1, tiled=True),
        lax.all_gather(value_projection, "ctx", axis=1, tiled=True),
        lax.all_gather(w_out, "ctx", axis=2, tiled=True),
    )
    query_weight = w_query[0]
    key_matrix = key_full[0]
    value_matrix = value_full[0]
    out_weight = out_part[0]
    tok_rows = half_rows * tp_count
    gain_row = norm_gain[0]
    query_heads = query_weight.shape[1] // HEAD_SIZE
    kv_heads = key_matrix.shape[1] // HEAD_SIZE
    group_size = query_heads // kv_heads
    reach_hops = min(-(-WINDOW // tok_rows), ctx_count - 1)
    token_index = ctx_num * tok_rows + jnp.arange(tok_rows, dtype=jnp.int32)
    key_index = (ctx_num - reach_hops) * tok_rows + jnp.arange(
        (reach_hops + 1) * tok_rows, dtype=jnp.int32
    )

    def project(operands):
        whole_rows, token_position = operands
        normalized_input = rms_normed(whole_rows, gain_row)
        query_matrix_rows = rotary_apply(
            jnp.dot(normalized_input, query_weight, preferred_element_type=jnp.float32).reshape(
                tok_rows, query_heads, HEAD_SIZE
            ),
            token_position,
        )
        key_matrix_rows = rotary_apply(
            jnp.dot(normalized_input, key_matrix, preferred_element_type=jnp.float32).reshape(
                tok_rows, kv_heads, HEAD_SIZE
            ),
            token_position,
        )
        value_rows = jnp.dot(
            normalized_input, value_matrix, preferred_element_type=jnp.float32
        ).astype(jnp.bfloat16)
        stacked = jnp.stack(
            [
                key_matrix_rows.astype(jnp.bfloat16).reshape(tok_rows, kv_heads * HEAD_SIZE),
                value_rows,
            ]
        )
        return (
            query_matrix_rows.astype(jnp.bfloat16).reshape(tok_rows, query_heads * HEAD_SIZE),
            stacked,
        )

    def skip_project(operands):
        return (
            jnp.zeros((tok_rows, query_heads * HEAD_SIZE), jnp.bfloat16),
            jnp.zeros((2, tok_rows, kv_heads * HEAD_SIZE), jnp.bfloat16),
        )

    def skip_attend(operands):
        return jnp.zeros((tok_rows, query_heads * HEAD_SIZE), jnp.bfloat16)

    def out_local(operands):
        return jnp.dot(operands, out_weight, preferred_element_type=jnp.float32)

    def skip_out(operands):
        return jnp.zeros((operands.shape[0], out_weight.shape[1]), jnp.float32)

    def step(step_num, carry):
        received, results = carry
        micro_num = step_num - section_num
        active = (micro_num >= 0) & (micro_num < micro_count)
        micro_at = jnp.clip(micro_num, 0, micro_count - 1)
        fresh_rows = lax.dynamic_index_in_dim(x_in, micro_at, 0, keepdims=False)
        current = jnp.where(section_num == 0, fresh_rows, received)
        whole_rows = lax.all_gather(current, "tp", axis=0, tiled=True)
        ids_row = lax.dynamic_index_in_dim(doc_ids, micro_at, 0, keepdims=False)
        token_position, query_doc = doc_lookup(ids_row, token_index, BLOCK)
        unused, key_doc = doc_lookup(ids_row, key_index, BLOCK)
        query_matrix_rows, stacked = lax.cond(
            active, project, skip_project, (whole_rows, token_position)
        )
        pieces = [shifted(stacked, "ctx", distance) for distance in range(reach_hops, 0, -1)]
        window_kv = jnp.concatenate(pieces + [stacked], axis=1)

        def attend(operands):
            query_part, window_part = operands
            grouped_heads = query_part.reshape(tok_rows, kv_heads, group_size, HEAD_SIZE)
            key_matrix_rows = window_part[0].reshape(-1, kv_heads, HEAD_SIZE)
            value_rows = window_part[1].reshape(-1, kv_heads, HEAD_SIZE)
            return attention_rows(
                grouped_heads,
                key_matrix_rows,
                value_rows,
                token_index,
                query_doc,
                key_index,
                key_doc,
            )

        attended = lax.cond(active, attend, skip_attend, (query_matrix_rows, window_kv))
        summed = lax.psum_scatter(
            lax.cond(active, out_local, skip_out, attended), "tp", scatter_dimension=0, tiled=True
        )
        updated = (current.astype(jnp.float32) + summed).astype(jnp.bfloat16)
        previous = lax.dynamic_index_in_dim(results, micro_at, 0, keepdims=False)
        results = lax.dynamic_update_index_in_dim(
            results, jnp.where(active, updated, previous), micro_at, 0
        )
        received = shifted(updated, "section", 1)
        return (received, results)

    start_carry = (
        jnp.zeros((half_rows, model_width), jnp.bfloat16),
        jnp.zeros((micro_count, half_rows, model_width), jnp.bfloat16),
    )
    unused_received, results = lax.fori_loop(0, micro_count + section_count - 1, step, start_carry)
    return results[None]


def solution(mesh):
    in_specs = (
        P(None, ("ctx", "tp"), None),
        P("section", None),
        P("section", None, "tp"),
        P("section", "ctx", "tp"),
        P("section", "ctx", "tp"),
        P("section", "tp", "ctx"),
        P(),
    )
    out_specs = P("section", None, ("ctx", "tp"), None)
    return jax.shard_map(local, mesh=mesh, in_specs=in_specs, out_specs=out_specs, check_vma=False)
```

profile of v0, /device:TPU:0, one launch (start us, length us, event | category | flops | bytes accessed | tf_op | source)
XLA Modules:
  0.0 705.6 jit_solution(9934352147820478738)
XLA Ops:
  9.5 60.5 %all-gather.9.cloned.1.call-done = bf16[1,1024,2688]{1,2,0:T(8,128)(2,1)} async-done(((bf16[1,1024,336]{1,2,0:T(8,128)(2,1)}), bf16[1,1024,2688]{1,2,0:T(8,128)(2,1)}) %all-gather.9.cloned.1.call-update) | async-done | bytes 5505040 | tf_op jit(solution)/shard_map/all_gather | solution.py:93
  70.0 8.3 %copy.36 = bf16[1024,2688]{1,0:T(8,128)(2,1)} copy(bf16[1024,2688]{0,1:T(8,128)(2,1)} %bitcast.77) | data formatting | bytes 11010048
  78.3 27.1 %all-gather.5.cloned.1.call-done = bf16[1,2688,512]{2,1,0:T(8,128)(2,1)} async-done(((bf16[1,336,512]{2,1,0:T(8,128)(2,1)}), bf16[1,2688,512]{2,1,0:T(8,128)(2,1)}) %all-gather.5.cloned.1.call-update) | async-done | bytes 2752528 | tf_op jit(solution)/shard_map/all_gather | solution.py:91
  105.4 35.6 %all-gather.7.cloned.1.call-done = bf16[1,2688,512]{2,1,0:T(8,128)(2,1)} async-done(((bf16[1,336,512]{2,1,0:T(8,128)(2,1)}), bf16[1,2688,512]{2,1,0:T(8,128)(2,1)}) %all-gather.7.cloned.1.call-update) | async-done | bytes 2752528 | tf_op jit(solution)/shard_map/all_gather | solution.py:92
  142.2 556.8 %while.20 = (s32[]{:T(128)}, bf16[128,2688]{1,0:T(8,128)(2,1)S(1)}, bf16[2,128,2688]{2,1,0:T(8,128)(2,1)}, pred[]{:T(512)}, s32[]{:T(128)}, /*index=5*/bf16[2,12...) while((s32[]{:T(128)}, bf16[128,2688]{1,0:T(8,128)(2,1)S(1)}, ...), condition=%wide.region_15.16_spmd.clone.clone, body=%wide.region_0.15_spmd.clone.clone.sunk | while | flops 6282989568 | bytes 119779400 | solution.py:202
  144.6 23.9 %all-gather.11.cloned.1.call-done = bf16[256,2688]{1,0:T(8,128)(2,1)} async-done(((bf16[128,2688]{1,0:T(8,128)(2,1)}), bf16[256,2688]{1,0:T(8,128)(2,1)}) %all-gather.11.cloned.1.call-update) | async-done | bytes 1376272 | tf_op jit(solution)/shard_map/while/body/eval_jaxpr/all_gather | solution.py:161
  168.4 16.0 %conditional.12 = (bf16[256,1024]{1,0:T(8,128)(2,1)}, bf16[2,256,512]{1,2,0:T(8,128)(2,1)S(1)}) conditional(s32[]{:T(128)} %convert_element_type.147, () %tuple.118, (bf16[256,2688]{1,0:T(8,128)(2,1)}, bf16[2688]{0:T(1024)(128)(2,1)S(1)}, bf16[2688,1024]{1,0:T(8,128)(2,1)}, s32[16,16]{1,0:T(8,128)S(1)}, pred[256,16]{0,1:T(8,128)(4,1)S(1)}, ...), branch_computations={%region_1.1_spmd, %region_2.5_spmd} | conditional | flops 2832461568 | bytes 35078064 | solution.py:165
  170.2 3.2 fusion.17
  175.3 2.7 fusion.15
  178.3 4.3 convolution_bitcast_fusion
  184.5 4.3 collective-permute-start
  188.8 2.6 collective-permute-start.1
  195.4 5.7 collective-permute-done
  201.2 11.2 %collective-permute-done.1 = bf16[2,256,512]{1,2,0:T(8,128)(2,1)S(1)} collective-permute-done((bf16[2,256,512]{1,2,0:T(8,128)(2,1)S(1)}, bf16[2,256,512]{1,2,0:T(8,128)(2,1)S(1)}, u32[]{:S(2)}, u32[]{:S(2)}) %collective-permute-start.1) | collective-permute-done | bytes 524320 | tf_op jit(solution)/shard_map/while/body/eval_jaxpr/ppermute | solution.py:18
  212.4 11.2 %collective-permute-done.2 = bf16[2,256,512]{1,2,0:T(8,128)(2,1)S(1)} collective-permute-done((bf16[2,256,512]{1,2,0:T(8,128)(2,1)S(1)}, bf16[2,256,512]{1,2,0:T(8,128)(2,1)S(1)}, u32[]{:S(2)}, u32[]{:S(2)}) %collective-permute-start.2) | collective-permute-done | bytes 524320 | tf_op jit(solution)/shard_map/while/body/eval_jaxpr/ppermute | solution.py:18
  223.8 16.1 %conditional.13 = (bf16[256,1024]{0,1:T(8,128)(2,1)S(1)}) conditional(s32[]{:T(128)} %convert_element_type.147, () %tuple.117, (s32[1280]{0:T(1024)S(1)}, s32[256]{0:T(256)S(1)}, s32[1280,1]{0,1:T(1,128)S(1)}, s32[1280]{0:T(1024)S(1)}, s32[1280,1]{0,1:T(1,128)S(1)}, /*index=5*/s32[]{:T(128)}, s32[1280,16]{0,1:T(8,128)S(1)}, ...), branch_computations={%region_6.6_spmd, %region_7.11_spmd.clone.clone} | conditional | flops 2039509248 | bytes 19503812 | solution.py:186
  228.2 5.1 fusion.52
  233.3 6.6 fusion.28
  239.9 4.3 conditional.14
  239.9 4.3 fusion.55
  246.9 58.4 %reduce-scatter.2.cloned.1.call-done = f32[128,2688]{1,0:T(8,128)} async-done(((f32[256,2688]{1,0:T(8,128)}), f32[128,2688]{1,0:T(8,128)}) %reduce-scatter.2.cloned.1.call-update) | async-done | bytes 1376272 | tf_op jit(solution)/shard_map/while/body/eval_jaxpr/reduce_scatter | solution.py:187
  307.8 3.4 collective-permute-start.4
  311.2 14.7 %collective-permute-done.4 = bf16[128,2688]{1,0:T(8,128)(2,1)S(1)} collective-permute-done((bf16[128,2688]{1,0:T(8,128)(2,1)S(1)}, bf16[128,2688]{1,0:T(8,128)(2,1)S(1)}, u32[]{:S(2)}, u32[]{:S(2)}) %collective-permute-start.4) | collective-permute-done | bytes 688160 | tf_op jit(solution)/shard_map/while/body/eval_jaxpr/ppermute | solution.py:18
  328.1 25.9 %all-gather.11.cloned.1.call-done = bf16[256,2688]{1,0:T(8,128)(2,1)} async-done(((bf16[128,2688]{1,0:T(8,128)(2,1)}), bf16[256,2688]{1,0:T(8,128)(2,1)}) %all-gather.11.cloned.1.call-update) | async-done | bytes 1376272 | tf_op jit(solution)/shard_map/while/body/eval_jaxpr/all_gather | solution.py:161
  354.0 16.0 %conditional.12 = (bf16[256,1024]{1,0:T(8,128)(2,1)}, bf16[2,256,512]{1,2,0:T(8,128)(2,1)S(1)}) conditional(s32[]{:T(128)} %convert_element_type.147, () %tuple.118, (bf16[256,2688]{1,0:T(8,128)(2,1)}, bf16[2688]{0:T(1024)(128)(2,1)S(1)}, bf16[2688,1024]{1,0:T(8,128)(2,1)}, s32[16,16]{1,0:T(8,128)S(1)}, pred[256,16]{0,1:T(8,128)(4,1)S(1)}, ...), branch_computations={%region_1.1_spmd, %region_2.5_spmd} | conditional | flops 2832461568 | bytes 35078064 | solution.py:165
  355.8 3.2 fusion.17
  360.9 2.7 fusion.15
  363.9 4.3 convolution_bitcast_fusion
  370.1 4.3 collective-permute-start
  381.0 5.7 collective-permute-done
  386.8 11.2 %collective-permute-done.1 = bf16[2,256,512]{1,2,0:T(8,128)(2,1)S(1)} collective-permute-done((bf16[2,256,512]{1,2,0:T(8,128)(2,1)S(1)}, bf16[2,256,512]{1,2,0:T(8,128)(2,1)S(1)}, u32[]{:S(2)}, u32[]{:S(2)}) %collective-permute-start.1) | collective-permute-done | bytes 524320 | tf_op jit(solution)/shard_map/while/body/eval_jaxpr/ppermute | solution.py:18
  398.0 11.2 %collective-permute-done.2 = bf16[2,256,512]{1,2,0:T(8,128)(2,1)S(1)} collective-permute-done((bf16[2,256,512]{1,2,0:T(8,128)(2,1)S(1)}, bf16[2,256,512]{1,2,0:T(8,128)(2,1)S(1)}, u32[]{:S(2)}, u32[]{:S(2)}) %collective-permute-start.2) | collective-permute-done | bytes 524320 | tf_op jit(solution)/shard_map/while/body/eval_jaxpr/ppermute | solution.py:18
  409.4 16.1 %conditional.13 = (bf16[256,1024]{0,1:T(8,128)(2,1)S(1)}) conditional(s32[]{:T(128)} %convert_element_type.147, () %tuple.117, (s32[1280]{0:T(1024)S(1)}, s32[256]{0:T(256)S(1)}, s32[1280,1]{0,1:T(1,128)S(1)}, s32[1280]{0:T(1024)S(1)}, s32[1280,1]{0,1:T(1,128)S(1)}, /*index=5*/s32[]{:T(128)}, s32[1280,16]{0,1:T(8,128)S(1)}, ...), branch_computations={%region_6.6_spmd, %region_7.11_spmd.clone.clone} | conditional | flops 2039509248 | bytes 19503812 | solution.py:186
  413.8 5.1 fusion.52
  418.9 6.6 fusion.28
  425.5 4.3 conditional.14
  425.5 4.3 fusion.55
  432.5 59.4 %reduce-scatter.2.cloned.1.call-done = f32[128,2688]{1,0:T(8,128)} async-done(((f32[256,2688]{1,0:T(8,128)}), f32[128,2688]{1,0:T(8,128)}) %reduce-scatter.2.cloned.1.call-update) | async-done | bytes 1376272 | tf_op jit(solution)/shard_map/while/body/eval_jaxpr/reduce_scatter | solution.py:187
  494.3 3.4 collective-permute-start.4
  497.7 14.6 %collective-permute-done.4 = bf16[128,2688]{1,0:T(8,128)(2,1)S(1)} collective-permute-done((bf16[128,2688]{1,0:T(8,128)(2,1)S(1)}, bf16[128,2688]{1,0:T(8,128)(2,1)S(1)}, u32[]{:S(2)}, u32[]{:S(2)}) %collective-permute-start.4) | collective-permute-done | bytes 688160 | tf_op jit(solution)/shard_map/while/body/eval_jaxpr/ppermute | solution.py:18
  514.6 26.1 %all-gather.11.cloned.1.call-done = bf16[256,2688]{1,0:T(8,128)(2,1)} async-done(((bf16[128,2688]{1,0:T(8,128)(2,1)}), bf16[256,2688]{1,0:T(8,128)(2,1)}) %all-gather.11.cloned.1.call-update) | async-done | bytes 1376272 | tf_op jit(solution)/shard_map/while/body/eval_jaxpr/all_gather | solution.py:161
  541.7 4.3 collective-permute-start
  552.6 5.7 collective-permute-done
  558.4 11.2 %collective-permute-done.1 = bf16[2,256,512]{1,2,0:T(8,128)(2,1)S(1)} collective-permute-done((bf16[2,256,512]{1,2,0:T(8,128)(2,1)S(1)}, bf16[2,256,512]{1,2,0:T(8,128)(2,1)S(1)}, u32[]{:S(2)}, u32[]{:S(2)}) %collective-permute-start.1) | collective-permute-done | bytes 524320 | tf_op jit(solution)/shard_map/while/body/eval_jaxpr/ppermute | solution.py:18
  569.6 11.2 %collective-permute-done.2 = bf16[2,256,512]{1,2,0:T(8,128)(2,1)S(1)} collective-permute-done((bf16[2,256,512]{1,2,0:T(8,128)(2,1)S(1)}, bf16[2,256,512]{1,2,0:T(8,128)(2,1)S(1)}, u32[]{:S(2)}, u32[]{:S(2)}) %collective-permute-start.2) | collective-permute-done | bytes 524320 | tf_op jit(solution)/shard_map/while/body/eval_jaxpr/ppermute | solution.py:18
  584.0 94.6 %reduce-scatter.2.cloned.1.call-done = f32[128,2688]{1,0:T(8,128)} async-done(((f32[256,2688]{1,0:T(8,128)}), f32[128,2688]{1,0:T(8,128)}) %reduce-scatter.2.cloned.1.call-update) | async-done | bytes 1376272 | tf_op jit(solution)/shard_map/while/body/eval_jaxpr/reduce_scatter | solution.py:187
  681.0 3.4 collective-permute-start.4
  684.4 14.6 %collective-permute-done.4 = bf16[128,2688]{1,0:T(8,128)(2,1)S(1)} collective-permute-done((bf16[128,2688]{1,0:T(8,128)(2,1)S(1)}, bf16[128,2688]{1,0:T(8,128)(2,1)S(1)}, u32[]{:S(2)}, u32[]{:S(2)}) %collective-permute-start.4) | collective-permute-done | bytes 688160 | tf_op jit(solution)/shard_map/while/body/eval_jaxpr/ppermute | solution.py:18
  (169 shorter events, 66.4 us)
Async XLA Ops:
  6.5 63.4 %all-gather.9.cloned.1.call-start = ((), (), s32[]{:S(2)}) async-start(), calls=%async_computation.3 | async-start | bytes 6193152 | tf_op jit(solution)/shard_map/all_gather | solution.py:93
  7.3 98.1 %all-gather.5.cloned.1.call-start = ((), (), s32[]{:S(2)}) async-start(), calls=%async_computation.1 | async-start | bytes 3096576 | tf_op jit(solution)/shard_map/all_gather | solution.py:91
  8.0 133.0 %all-gather.7.cloned.1.call-start = ((), (), s32[]{:S(2)}) async-start(), calls=%async_computation.2 | async-start | bytes 3096576 | tf_op jit(solution)/shard_map/all_gather | solution.py:92
  70.0 72.3 %copy-start.5 = (s32[2,16]{1,0:T(2,128)S(1)}, s32[2,16]{1,0:T(2,128)}, u32[]{:S(2)}) copy-start(s32[2,16]{1,0:T(2,128)} %param.21) | copy-start | bytes 388
  142.2 26.2 %all-gather.11.cloned.1.call-start = ((), (), s32[]{:S(2)}) async-start(), calls=%async_computation.4 | async-start | bytes 2064384 | tf_op jit(solution)/shard_map/while/body/eval_jaxpr/all_gather | solution.py:161
  144.4 161.0 %reduce-scatter.2.cloned.1.call-start = ((), (), s32[]{:S(2)}) async-start(), calls=%async_computation.5 | async-start | bytes 4128768 | tf_op jit(solution)/shard_map/while/body/eval_jaxpr/reduce_scatter | solution.py:187
  173.3 1.9 copy-start.2
  184.5 16.7 %collective-permute-start = (bf16[2,256,512]{1,2,0:T(8,128)(2,1)S(1)}, bf16[2,256,512]{1,2,0:T(8,128)(2,1)S(1)}, u32[]{:S(2)}, u32[]{:S(2)}) collective-permute-start(bf16[2,256,512]{1,2,0:T(8,128)(2,1)S(1)} %get-tuple-element.916), channel_id=1, source_target_pairs={{0,8},{2,10},{4,12},{6,14},{1,9},{3,11},{5,13},{7,15},{16,24},{18,... | collective-permute-start | bytes 1572872 | tf_op jit(solution)/shard_map/while/body/eval_jaxpr/ppermute | solution.py:18
  188.8 23.6 %collective-permute-start.1 = (bf16[2,256,512]{1,2,0:T(8,128)(2,1)S(1)}, bf16[2,256,512]{1,2,0:T(8,128)(2,1)S(1)}, u32[]{:S(2)}, u32[]{:S(2)}) collective-permute-start(bf16[2,256,512]{1,2,0:T(8,128)(2,1)S(1)} %get-tuple-element.916), channel_id=1, source_target_pairs={{0,6},{2,8},{4,10},{6,12},{8,14},{1,7},{3,9},{5,11},{7,13},{9,15},... | collective-permute-start | bytes 1572872 | tf_op jit(solution)/shard_map/while/body/eval_jaxpr/ppermute | solution.py:18
  191.4 32.2 %collective-permute-start.2 = (bf16[2,256,512]{1,2,0:T(8,128)(2,1)S(1)}, bf16[2,256,512]{1,2,0:T(8,128)(2,1)S(1)}, u32[]{:S(2)}, u32[]{:S(2)}) collective-permute-start(bf16[2,256,512]{1,2,0:T(8,128)(2,1)S(1)} %get-tuple-element.916), channel_id=1, source_target_pairs={{0,4},{2,6},{4,8},{6,10},{8,12},{10,14},{1,5},{3,7},{5,9},{7,11},{... | collective-permute-start | bytes 1572872 | tf_op jit(solution)/shard_map/while/body/eval_jaxpr/ppermute | solution.py:18
  193.6 30.1 %collective-permute-start.3 = (bf16[2,256,512]{1,2,0:T(8,128)(2,1)S(1)}, bf16[2,256,512]{1,2,0:T(8,128)(2,1)S(1)}, u32[]{:S(2)}, u32[]{:S(2)}) collective-permute-start(bf16[2,256,512]{1,2,0:T(8,128)(2,1)S(1)} %get-tuple-element.916), channel_id=1, source_target_pairs={{0,2},{2,4},{4,6},{6,8},{8,10},{10,12},{12,14},{1,3},{3,5},{5,7},{... | collective-permute-start | bytes 1572872 | tf_op jit(solution)/shard_map/while/body/eval_jaxpr/ppermute | solution.py:18
  225.1 3.1 copy-start.4
  228.2 5.1 copy-start.3
  244.2 1.5 copy-start
  244.2 61.1 %copy-start.1 = (bf16[128,2688]{1,0:T(8,128)(2,1)S(1)}, bf16[128,2688]{1,0:T(8,128)(2,1)}, u32[]{:S(2)}) copy-start(bf16[128,2688]{1,0:T(8,128)(2,1)} %bitcast_select_fusion.9) | copy-start | bytes 2064388 | tf_op jit(solution)/shard_map/while
  307.8 18.1 %collective-permute-start.4 = (bf16[128,2688]{1,0:T(8,128)(2,1)S(1)}, bf16[128,2688]{1,0:T(8,128)(2,1)S(1)}, u32[]{:S(2)}, u32[]{:S(2)}) collective-permute-start(bf16[128,2688]{1,0:T(8,128)(2,1)S(1)} %get-tuple-element.918), channel_id=1, source_target_pairs={{0,16},{1,17},{2,18},{3,19},{4,20},{5,21},{6,22},{7,23},{8,24},{9,... | collective-permute-start | bytes 2064392 | tf_op jit(solution)/shard_map/while/body/eval_jaxpr/ppermute | solution.py:18
  325.8 28.2 %all-gather.11.cloned.1.call-start = ((), (), s32[]{:S(2)}) async-start(), calls=%async_computation.4 | async-start | bytes 2064384 | tf_op jit(solution)/shard_map/while/body/eval_jaxpr/all_gather | solution.py:161
  327.9 164.0 %reduce-scatter.2.cloned.1.call-start = ((), (), s32[]{:S(2)}) async-start(), calls=%async_computation.5 | async-start | bytes 4128768 | tf_op jit(solution)/shard_map/while/body/eval_jaxpr/reduce_scatter | solution.py:187
  358.9 1.9 copy-start.2
  370.1 16.7 %collective-permute-start = (bf16[2,256,512]{1,2,0:T(8,128)(2,1)S(1)}, bf16[2,256,512]{1,2,0:T(8,128)(2,1)S(1)}, u32[]{:S(2)}, u32[]{:S(2)}) collective-permute-start(bf16[2,256,512]{1,2,0:T(8,128)(2,1)S(1)} %get-tuple-element.916), channel_id=1, source_target_pairs={{0,8},{2,10},{4,12},{6,14},{1,9},{3,11},{5,13},{7,15},{16,24},{18,... | collective-permute-start | bytes 1572872 | tf_op jit(solution)/shard_map/while/body/eval_jaxpr/ppermute | solution.py:18
  374.4 23.6 %collective-permute-start.1 = (bf16[2,256,512]{1,2,0:T(8,128)(2,1)S(1)}, bf16[2,256,512]{1,2,0:T(8,128)(2,1)S(1)}, u32[]{:S(2)}, u32[]{:S(2)}) collective-permute-start(bf16[2,256,512]{1,2,0:T(8,128)(2,1)S(1)} %get-tuple-element.916), channel_id=1, source_target_pairs={{0,6},{2,8},{4,10},{6,12},{8,14},{1,7},{3,9},{5,11},{7,13},{9,15},... | collective-permute-start | bytes 1572872 | tf_op jit(solution)/shard_map/while/body/eval_jaxpr/ppermute | solution.py:18
  377.0 32.2 %collective-permute-start.2 = (bf16[2,256,512]{1,2,0:T(8,128)(2,1)S(1)}, bf16[2,256,512]{1,2,0:T(8,128)(2,1)S(1)}, u32[]{:S(2)}, u32[]{:S(2)}) collective-permute-start(bf16[2,256,512]{1,2,0:T(8,128)(2,1)S(1)} %get-tuple-element.916), channel_id=1, source_target_pairs={{0,4},{2,6},{4,8},{6,10},{8,12},{10,14},{1,5},{3,7},{5,9},{7,11},{... | collective-permute-start | bytes 1572872 | tf_op jit(solution)/shard_map/while/body/eval_jaxpr/ppermute | solution.py:18
  379.2 30.1 %collective-permute-start.3 = (bf16[2,256,512]{1,2,0:T(8,128)(2,1)S(1)}, bf16[2,256,512]{1,2,0:T(8,128)(2,1)S(1)}, u32[]{:S(2)}, u32[]{:S(2)}) collective-permute-start(bf16[2,256,512]{1,2,0:T(8,128)(2,1)S(1)} %get-tuple-element.916), channel_id=1, source_target_pairs={{0,2},{2,4},{4,6},{6,8},{8,10},{10,12},{12,14},{1,3},{3,5},{5,7},{... | collective-permute-start | bytes 1572872 | tf_op jit(solution)/shard_map/while/body/eval_jaxpr/ppermute | solution.py:18
  410.7 3.1 copy-start.4
  413.8 5.1 copy-start.3
  429.8 1.5 copy-start
  429.8 62.1 %copy-start.1 = (bf16[128,2688]{1,0:T(8,128)(2,1)S(1)}, bf16[128,2688]{1,0:T(8,128)(2,1)}, u32[]{:S(2)}) copy-start(bf16[128,2688]{1,0:T(8,128)(2,1)} %bitcast_select_fusion.9) | copy-start | bytes 2064388 | tf_op jit(solution)/shard_map/while
  494.3 18.0 %collective-permute-start.4 = (bf16[128,2688]{1,0:T(8,128)(2,1)S(1)}, bf16[128,2688]{1,0:T(8,128)(2,1)S(1)}, u32[]{:S(2)}, u32[]{:S(2)}) collective-permute-start(bf16[128,2688]{1,0:T(8,128)(2,1)S(1)} %get-tuple-element.918), channel_id=1, source_target_pairs={{0,16},{1,17},{2,18},{3,19},{4,20},{5,21},{6,22},{7,23},{8,24},{9,... | collective-permute-start | bytes 2064392 | tf_op jit(solution)/shard_map/while/body/eval_jaxpr/ppermute | solution.py:18
  512.3 28.4 %all-gather.11.cloned.1.call-start = ((), (), s32[]{:S(2)}) async-start(), calls=%async_computation.4 | async-start | bytes 2064384 | tf_op jit(solution)/shard_map/while/body/eval_jaxpr/all_gather | solution.py:161
  514.4 164.2 %reduce-scatter.2.cloned.1.call-start = ((), (), s32[]{:S(2)}) async-start(), calls=%async_computation.5 | async-start | bytes 4128768 | tf_op jit(solution)/shard_map/while/body/eval_jaxpr/reduce_scatter | solution.py:187
  541.7 16.7 %collective-permute-start = (bf16[2,256,512]{1,2,0:T(8,128)(2,1)S(1)}, bf16[2,256,512]{1,2,0:T(8,128)(2,1)S(1)}, u32[]{:S(2)}, u32[]{:S(2)}) collective-permute-start(bf16[2,256,512]{1,2,0:T(8,128)(2,1)S(1)} %get-tuple-element.916), channel_id=1, source_target_pairs={{0,8},{2,10},{4,12},{6,14},{1,9},{3,11},{5,13},{7,15},{16,24},{18,... | collective-permute-start | bytes 1572872 | tf_op jit(solution)/shard_map/while/body/eval_jaxpr/ppermute | solution.py:18
  546.0 23.6 %collective-permute-start.1 = (bf16[2,256,512]{1,2,0:T(8,128)(2,1)S(1)}, bf16[2,256,512]{1,2,0:T(8,128)(2,1)S(1)}, u32[]{:S(2)}, u32[]{:S(2)}) collective-permute-start(bf16[2,256,512]{1,2,0:T(8,128)(2,1)S(1)} %get-tuple-element.916), channel_id=1, source_target_pairs={{0,6},{2,8},{4,10},{6,12},{8,14},{1,7},{3,9},{5,11},{7,13},{9,15},... | collective-permute-start | bytes 1572872 | tf_op jit(solution)/shard_map/while/body/eval_jaxpr/ppermute | solution.py:18
  548.6 32.2 %collective-permute-start.2 = (bf16[2,256,512]{1,2,0:T(8,128)(2,1)S(1)}, bf16[2,256,512]{1,2,0:T(8,128)(2,1)S(1)}, u32[]{:S(2)}, u32[]{:S(2)}) collective-permute-start(bf16[2,256,512]{1,2,0:T(8,128)(2,1)S(1)} %get-tuple-element.916), channel_id=1, source_target_pairs={{0,4},{2,6},{4,8},{6,10},{8,12},{10,14},{1,5},{3,7},{5,9},{7,11},{... | collective-permute-start | bytes 1572872 | tf_op jit(solution)/shard_map/while/body/eval_jaxpr/ppermute | solution.py:18
  550.8 30.1 %collective-permute-start.3 = (bf16[2,256,512]{1,2,0:T(8,128)(2,1)S(1)}, bf16[2,256,512]{1,2,0:T(8,128)(2,1)S(1)}, u32[]{:S(2)}, u32[]{:S(2)}) collective-permute-start(bf16[2,256,512]{1,2,0:T(8,128)(2,1)S(1)} %get-tuple-element.916), channel_id=1, source_target_pairs={{0,2},{2,4},{4,6},{6,8},{8,10},{10,12},{12,14},{1,3},{3,5},{5,7},{... | collective-permute-start | bytes 1572872 | tf_op jit(solution)/shard_map/while/body/eval_jaxpr/ppermute | solution.py:18
  581.2 1.5 copy-start
  581.2 97.3 %copy-start.1 = (bf16[128,2688]{1,0:T(8,128)(2,1)S(1)}, bf16[128,2688]{1,0:T(8,128)(2,1)}, u32[]{:S(2)}) copy-start(bf16[128,2688]{1,0:T(8,128)(2,1)} %bitcast_select_fusion.9) | copy-start | bytes 2064388 | tf_op jit(solution)/shard_map/while
  681.0 18.1 %collective-permute-start.4 = (bf16[128,2688]{1,0:T(8,128)(2,1)S(1)}, bf16[128,2688]{1,0:T(8,128)(2,1)S(1)}, u32[]{:S(2)}, u32[]{:S(2)}) collective-permute-start(bf16[128,2688]{1,0:T(8,128)(2,1)S(1)} %get-tuple-element.918), channel_id=1, source_target_pairs={{0,16},{1,17},{2,18},{3,19},{4,20},{5,21},{6,22},{7,23},{8,24},{9,... | collective-permute-start | bytes 2064392 | tf_op jit(solution)/shard_map/while/body/eval_jaxpr/ppermute | solution.py:18
Sparse Core Ops, SparseCore 0:
  9.0 60.9 all-gather.8
  71.6 33.7 all-gather.4
  107.0 33.9 all-gather.6
  144.5 23.9 all-gather.10
  245.9 59.4 reduce-scatter.1
  328.0 25.9 all-gather.10
  431.5 60.3 reduce-scatter.1
  514.7 25.9 all-gather.10
  582.9 95.5 reduce-scatter.1
where the time goes:
time: 707 us; the launch traced here: 706 us
  waiting for transfers between devices  542 us (77%)
  matrix products  52.2 us (7%)
  starting transfers between devices  43.2 us (6%)
  local copies, waits for them, and re-layouts  28.6 us (4%)
  other arithmetic  25.4 us (4%)
  between operations  13.1 us (2%)
    reduce_scatter x3, waiting for transfers between devices, step(): lax.psum_scatter(lax.cond(active, out_local, skip_out, attended), 'tp', s...  212 us
    ppermute x15, waiting for transfers between devices, shifted(): return lax.ppermute(shard, axis, pairs)  128 us
    all_gather x3, waiting for transfers between devices, step(): whole_rows = lax.all_gather(current, 'tp', axis=0, tiled=True)  75.9 us
    all_gather x1, waiting for transfers between devices, local(): lax.all_gather(w_out, 'ctx', axis=2, tiled=True)  60.5 us
    ppermute x15, starting transfers between devices, shifted(): return lax.ppermute(shard, axis, pairs)  42.9 us
    all_gather x1, waiting for transfers between devices, local(): lax.all_gather(value_projection, 'ctx', axis=1, tiled=True)  35.6 us
    all_gather x1, waiting for transfers between devices, local(): lax.all_gather(w_key, 'ctx', axis=1, tiled=True)  27.1 us
  transfers between devices with their start and end apart: 24, of which 21 were waited for; matrix products, arithmetic and copies ran while one was open for 2% of the time, Pallas kernels for 0%

commit v1 on v0

--- a/solution.py
+++ b/solution.py
@@ -1,6 +1,8 @@
 import jax
 import jax.numpy as jnp
 from jax import lax
+from jax.experimental import pallas as pl
+from jax.experimental.pallas import tpu as pltpu
 from jax.sharding import PartitionSpec as P
 
 HEAD_SIZE = 128
@@ -203,6 +205,283 @@
     return results[None]
 
 
+LANES = 128
+
+
+def swapped(shard, axis):
+    return lax.ppermute(shard, axis, [(0, 1), (1, 0)])
+
+
+def core_swapped(shard, ctx_count):
+    return lax.ppermute(shard, "ctx", [(i, i ^ 1) for i in range(ctx_count)])
+
+
+def chip_xor(shard, ctx_count, by):
+    return lax.ppermute(shard, "ctx", [(i, i ^ (2 * by)) for i in range(ctx_count)])
+
+
+def chip_shift(shard, ctx_count, by):
+    return lax.ppermute(
+        shard, "ctx", [(i, i + 2 * by) for i in range(ctx_count) if i + 2 * by < ctx_count]
+    )
+
+
+def columns(array, block, width):
+    return lax.dynamic_slice_in_dim(array, block * width, width, 1)
+
+
+def own_first(flag, own, other):
+    return jnp.where(flag == 0, own, other), jnp.where(flag == 0, other, own)
+
+
+def attention_kernel(low_ref, query_ref, far_ref, near_ref, own_ref, out_ref, window_ref):
+    size = HEAD_SIZE
+    window_ref[0:BLOCK, :] = far_ref[...]
+    for block in range(4):
+        at = (0, 2, 1, 3)[block] * BLOCK
+        window_ref[(1 + block) * BLOCK : (2 + block) * BLOCK, :] = near_ref[at : at + BLOCK, :]
+        window_ref[(5 + block) * BLOCK : (6 + block) * BLOCK, :] = own_ref[at : at + BLOCK, :]
+    span = 6 * BLOCK
+    row = lax.broadcasted_iota(jnp.int32, (2 * BLOCK, span), 0) % BLOCK
+    col = lax.broadcasted_iota(jnp.int32, (2 * BLOCK, span), 1)
+    causal = col - 5 * BLOCK <= row
+    for block in range(4):
+        at = (0, 2, 1, 3)[block] * BLOCK
+        rows = slice(block * BLOCK, (block + 6) * BLOCK)
+        query = jnp.concatenate(
+            [query_ref[at : at + BLOCK, 0:size], query_ref[at : at + BLOCK, size : 2 * size]], axis=0
+        )
+        scores = lax.dot_general(
+            query,
+            window_ref[rows, 0:size],
+            (((1,), (1,)), ((), ())),
+            preferred_element_type=jnp.float32,
+        )
+        allowed = causal & (col >= low_ref[block] * BLOCK)
+        scores = jnp.where(allowed, scores * query_scale, -1e30)
+        raised = jnp.exp(scores - jnp.max(scores, axis=-1, keepdims=True))
+        total = jnp.sum(raised, axis=-1, keepdims=True)
+        mixed = jnp.dot(
+            raised.astype(jnp.bfloat16),
+            window_ref[rows, size : 2 * size],
+            preferred_element_type=jnp.float32,
+        )
+        mixed = (mixed / total).astype(jnp.bfloat16)
+        out_ref[at : at + BLOCK, 0:size] = mixed[0:BLOCK]
+        out_ref[at : at + BLOCK, size : 2 * size] = mixed[BLOCK:]
+
+
+def attend_heads(low, query, far, near, own):
+    vmem = pl.BlockSpec(memory_space=pltpu.VMEM)
+    return pl.pallas_call(
+        attention_kernel,
+        out_shape=jax.ShapeDtypeStruct(query.shape, jnp.bfloat16),
+        in_specs=[pl.BlockSpec(memory_space=pltpu.SMEM), vmem, vmem, vmem, vmem],
+        out_specs=vmem,
+        scratch_shapes=[pltpu.VMEM((9 * BLOCK, 2 * HEAD_SIZE), jnp.bfloat16)],
+        compiler_params=pltpu.CompilerParams(vmem_limit_bytes=32 * 2**20),
+        cost_estimate=pl.CostEstimate(
+            flops=4 * 4 * 2 * BLOCK * 6 * BLOCK * HEAD_SIZE,
+            bytes_accessed=2 * 2**20,
+            transcendentals=4 * 2 * BLOCK * 6 * BLOCK,
+        ),
+    )(low, query, far, near, own)
+
+
+def split_heads(x_in, norm_gain, w_query, w_key, value_projection, w_out, doc_ids):
+    section = lax.axis_index("section")
+    ctx = lax.axis_index("ctx")
+    tp = lax.axis_index("tp")
+    ctx_count = lax.axis_size("ctx")
+    chips = ctx_count // 2
+    chip, core = ctx // 2, ctx % 2
+    micro_count, half_rows, width = x_in.shape
+    chip_rows = 4 * half_rows
+    slab = width // ctx_count
+    layers = range(2)
+    head = HEAD_SIZE
+
+    def of_core(which):
+        parts = []
+        for sec in (0, 1):
+            for weight in (w_key[0], value_projection[0]):
+                parts.append(columns(weight, sec * 2 + which, head))
+        return jnp.concatenate(parts, axis=1)
+
+    mine = of_core(core)
+    theirs = core_swapped(of_core(1 - core), ctx_count)
+    chip_kv = jnp.concatenate(own_first(core, mine, theirs), axis=0)
+    kv_own = columns(chip_kv, section, 2 * head)
+    kv_other = swapped(columns(chip_kv, 1 - section, 2 * head), "section")
+    kv_shards = own_first(section, kv_own, kv_other)
+    gains = own_first(section, norm_gain[0], swapped(norm_gain[0], "section"))
+
+    out_t = w_out[0].T
+    crossed = lax.ppermute(
+        out_t,
+        ("section", "ctx"),
+        [(s * ctx_count + i, (1 - s) * ctx_count + i) for s in (0, 1) for i in range(ctx_count) if i % 2 != s],
+    )
+    out_shards = own_first(section, out_t, crossed)
+
+    def gather_kv(shard):
+        whole = jnp.zeros((width, 2 * head), jnp.bfloat16)
+        for by in range(chips):
+            part = shard if by == 0 else chip_xor(shard, ctx_count, by)
+            whole = lax.dynamic_update_slice_in_dim(whole, part, (chip ^ by) * 2 * slab, 0)
+        return whole
+
+    def gather_out(shard):
+        got = [
+            lax.ppermute(
+                shard,
+                ("section", "ctx"),
+                [
+                    (s * ctx_count + 2 * i + s, s * ctx_count + 2 * (i ^ by) + i // 2)
+                    for s in (0, 1)
+                    for i in range(chips)
+                ],
+            )
+            for by in range(chips)
+        ]
+        high = (chip // 2) ^ core
+        even = jnp.where(high == 1, got[2], got[0])
+        odd = jnp.where(high == 1, got[3], got[1])
+        low = chip % 2
+        rows = jnp.concatenate(own_first(low, even, odd), axis=0)
+        me = 2 * section + core
+        return jnp.concatenate([columns(rows, me ^ by, 2 * head) for by in range(4)], axis=1)
+
+    block_count = doc_ids.shape[1]
+    start = jnp.sum((doc_ids[:, None, :] < doc_ids[:, :, None]).astype(jnp.int32), axis=2)
+    chip_start = lax.dynamic_slice_in_dim(start, chip * 4, 4, 1)
+    inside = chip * 4 + jnp.arange(4, dtype=jnp.int32)[None, :] - chip_start
+    lows = 5 - inside
+    order = inside.reshape(micro_count, 2, 2).transpose(0, 2, 1).reshape(micro_count, 4)
+    position = (order[:, :, None] * BLOCK + jnp.arange(BLOCK, dtype=jnp.int32)).reshape(
+        micro_count, chip_rows
+    )
+    half = head // 2
+    frequency = rope_base ** (-(jnp.arange(half, dtype=jnp.float32) * 2.0) / head)
+    angles = position.astype(jnp.float32)[:, :, None] * frequency
+    cosine, sine = jnp.cos(angles), jnp.sin(angles)
+    cosine = jnp.concatenate([cosine, cosine], axis=-1)
+    sine = jnp.concatenate([-sine, sine], axis=-1)
+
+    def rope(array, micro):
+        heads = []
+        for at in range(0, array.shape[1], head):
+            one = array[:, at : at + head]
+            turned = jnp.concatenate([one[:, half:], one[:, :half]], axis=1)
+            heads.append(one * cosine[micro] + turned * sine[micro])
+        return jnp.concatenate(heads, axis=1).astype(jnp.bfloat16)
+
+    def first_hidden(micro):
+        mine = x_in[micro].T
+        pair = jnp.concatenate(own_first(tp, mine, swapped(mine, "tp")), axis=1)
+        other = core_swapped(pair, ctx_count)
+        first, second = own_first(core, pair, other)
+        return jnp.concatenate(
+            [first[:, :half_rows], second[:, :half_rows], first[:, half_rows:], second[:, half_rows:]],
+            axis=1,
+        )
+
+    query_weight = jnp.concatenate(
+        [columns(w_query[0], sec * 2 + core, 2 * head) for sec in (0, 1)], axis=1
+    )
+
+    def tn(left, right):
+        return lax.dot_general(
+            left, right, (((0,), (0,)), ((), ())), preferred_element_type=jnp.float32
+        )
+
+    def project(layer, micro, hidden, kv_weight):
+        widened = hidden.astype(jnp.float32)
+        mean_square = jnp.mean(widened * widened, axis=0, keepdims=True)
+        normed = (
+            widened * lax.rsqrt(mean_square + 1e-06) * gains[layer].astype(jnp.float32)[:, None]
+        ).astype(jnp.bfloat16)
+        query = rope(tn(normed, query_weight), micro)
+        key_value = tn(normed, kv_weight)
+        key_value = jnp.concatenate(
+            [rope(key_value[:, :head], micro), key_value[:, head:].astype(jnp.bfloat16)], axis=1
+        )
+        sent = lax.ppermute(
+            columns(query, 1 - section, 2 * head), "section", [(layer, 1 - layer)]
+        )
+        query = jnp.where(section == layer, columns(query, section, 2 * head), sent)
+        near = chip_shift(key_value, ctx_count, 1)
+        far = chip_shift(key_value[3 * BLOCK :], ctx_count, 2)
+        return attend_heads(lows[micro], query, far, near, key_value)
+
+    def mix(layer, hidden, attended, out_weight):
+        across = swapped(attended, "section")
+        pair = jnp.concatenate([attended, across], axis=1)
+        four = core_swapped(pair, ctx_count)
+        every = jnp.concatenate(
+            [attended, four[:, : 2 * head], across, four[:, 2 * head :]], axis=1
+        )
+        partial = lax.dot_general(
+            out_weight, every, (((1,), (1,)), ((), ())), preferred_element_type=jnp.float32
+        )
+        half_tokens = chip_rows // 2
+        arrived = swapped(columns(partial, 1 - tp, half_tokens).astype(jnp.bfloat16), "tp")
+        mine = columns(hidden, tp, half_tokens)
+        residual = jnp.concatenate(
+            [
+                lax.dynamic_slice_in_dim(mine, (4 * core + section) * slab, slab, 0),
+                lax.dynamic_slice_in_dim(mine, (4 * core + 2 + section) * slab, slab, 0),
+            ],
+            axis=0,
+        ).astype(jnp.float32)
+        return (
+            residual + columns(partial, tp, half_tokens) + arrived.astype(jnp.float32)
+        ).astype(jnp.bfloat16)
+
+    def by_section(own, other):
+        first, second = own_first(section, own, other)
+        return jnp.concatenate(
+            [first[:slab], second[:slab], first[slab:], second[slab:]], axis=0
+        )
+
+    def spread(piece):
+        left, right = piece[:, :half_rows], piece[:, half_rows:]
+        left_x = swapped(left, "tp")
+        right_y = swapped(right, "section")
+        left_y = swapped(jnp.concatenate([left, left_x], axis=1), "section")
+        right_x = swapped(jnp.concatenate([right, right_y], axis=1), "tp")
+        here = by_section(piece, jnp.concatenate([left_y[:, :half_rows], right_y], axis=1))
+        there = by_section(
+            jnp.concatenate([left_x, right_x[:, :half_rows]], axis=1),
+            jnp.concatenate([left_y[:, half_rows:], right_x[:, half_rows:]], axis=1),
+        )
+        both = jnp.concatenate(own_first(tp, here, there), axis=1)
+        return jnp.concatenate(own_first(core, both, core_swapped(both, ctx_count)), axis=0)
+
+    def finish(piece):
+        got = lax.ppermute(piece, "section", [(0, 1)])
+        both = by_section(piece, got)
+        other = core_swapped(columns(both, 1 - core, half_rows), ctx_count)
+        return jnp.concatenate(own_first(core, columns(both, core, half_rows), other), axis=0).T
+
+    micros = range(micro_count)
+    hidden = [first_hidden(micro) for micro in micros]
+    results = []
+    for layer in layers:
+        kv_weight = gather_kv(kv_shards[layer])
+        out_weight = gather_out(out_shards[layer])
+        attended = [project(layer, micro, hidden[micro], kv_weight) for micro in micros]
+        pieces = [mix(layer, hidden[micro], attended[micro], out_weight) for micro in micros]
+        if layer == 0:
+            hidden = [spread(piece) for piece in pieces]
+            results.append(
+                jnp.stack([columns(one, 2 * tp + core, half_rows).T for one in hidden])
+            )
+        else:
+            results.append(jnp.stack([finish(piece) for piece in pieces]))
+    return jnp.where(section == 0, results[0], results[1])[None]
+
+
 def solution(mesh):
     in_specs = (
         P(None, ("ctx", "tp"), None),
@@ -214,4 +493,7 @@
         P(),
     )
     out_specs = P("section", None, ("ctx", "tp"), None)
-    return jax.shard_map(local, mesh=mesh, in_specs=in_specs, out_specs=out_specs, check_vma=False)
+    sizes = mesh.shape
+    fits = sizes["section"] == 2 and sizes["tp"] == 2 and sizes["ctx"] == 8
+    body = split_heads if fits else local
+    return jax.shard_map(body, mesh=mesh, in_specs=in_specs, out_specs=out_specs, check_vma=False)

time: 707 us -> 340 us (0.48)
  waiting for transfers between devices: 542 us -> 130 us
  starting transfers between devices: 43.2 us -> 134 us
  matrix products: 52.2 us -> 17.5 us
  local copies, waits for them, and re-layouts: 28.6 us -> 14.4 us
  between operations: 13.1 us -> 1.64 us
  Pallas kernels: 0 us -> 9.49 us
    reduce_scatter x3 -> x0, waiting for transfers between devices: 212 us -> none  [step(): lax.psum_scatter(lax.cond(active, out_local, skip_out, attended), 'tp', s...]
    all_gather x6 -> x0, waiting for transfers between devices: 199 us -> none  [the longest x3 75.9 us: step(): whole_rows = lax.all_gather(current, 'tp', axis=0, tiled=True)]
    ppermute x15 -> x60, starting transfers between devices: 42.9 us -> 134 us  [the longest x8 44.8 us: gather_out(): lax.ppermute(shard, ('section', 'ctx'), [(s * ctx_count + 2 * i + s, s *...]
    dot_general x10 -> x12, matrix products: 42 us -> 17.5 us  [the longest x8 13.8 us: tn(): lax.dot_general(left, right, (((0,), (0,)), ((), ())), preferred_element_...]
    sub x2 -> x0, matrix products: 10.3 us -> none  [attention_rows(): raised = jnp.exp(scores - peak_score)]
    pallas_call x0 -> x4, Pallas kernels: none -> 9.49 us  [attend_heads(): pl.pallas_call(attention_kernel, out_shape=jax.ShapeDtypeStruct(query.sha...]
    ppermute x15 -> x60, waiting for transfers between devices: 128 us -> 130 us  [the longest x20 82.4 us: swapped(): return lax.ppermute(shard, axis, [(0, 1), (1, 0)])]
  transfers between devices with their start and end apart: 24 -> 60, of which waited for: 21 -> 27; matrix products, arithmetic and copies ran while one was open for 2% -> 14% of each run, Pallas kernels for 0% -> 3%
where the time goes in v1:
time: 340 us; the launch traced here: 333 us
  starting transfers between devices  134 us (39%)
  waiting for transfers between devices  130 us (38%)
  other arithmetic  25.9 us (8%)
  matrix products  17.5 us (5%)
  local copies, waits for them, and re-layouts  14.4 us (4%)
  Pallas kernels  9.49 us (3%)
    ppermute x20, waiting for transfers between devices, swapped(): return lax.ppermute(shard, axis, [(0, 1), (1, 0)])  82.4 us
    ppermute x8, starting transfers between devices, gather_out(): lax.ppermute(shard, ('section', 'ctx'), [(s * ctx_count + 2 * i + s, s *...  44.8 us
    ppermute x8, starting transfers between devices, chip_shift(): lax.ppermute(shard, 'ctx', [(i, i + 2 * by) for i in range(ctx_count) if...  37.1 us
    ppermute x20, starting transfers between devices, swapped(): return lax.ppermute(shard, axis, [(0, 1), (1, 0)])  25.8 us
    ppermute x6, waiting for transfers between devices, chip_xor(): lax.ppermute(shard, 'ctx', [(i, i ^ 2 * by) for i in range(ctx_count)])  21.8 us
    dot_general x8, matrix products, tn(): lax.dot_general(left, right, (((0,), (0,)), ((), ())), preferred_element_...  13.8 us
    ppermute x6, starting transfers between devices, chip_xor(): lax.ppermute(shard, 'ctx', [(i, i ^ 2 * by) for i in range(ctx_count)])  10.8 us
    pallas_call x4, Pallas kernels, attend_heads(): pl.pallas_call(attention_kernel, out_shape=jax.ShapeDtypeStruct(query.sha...  9.49 us
  transfers between devices with their start and end apart: 60, of which 27 were waited for; matrix products, arithmetic and copies ran while one was open for 14% of the time, Pallas kernels for 3%

profile of v1, /device:TPU:0, one launch (start us, length us, event | category | flops | bytes accessed | tf_op | source)
XLA Modules:
  0.0 333.5 jit_solution(9081969775779048987)
XLA Ops:
  1.3 3.0 collective-permute-start.7
  4.3 2.0 dynamic-slice_bitcast_fusion.8
  11.4 2.9 multiply_cosine_fusion
  14.4 3.5 %dynamic-slice_bitcast_fusion.1 = (bf16[2688,256]{1,0:T(8,128)(2,1)}, bf16[2688,256]{1,0:T(8,128)(2,1)}) fusion(bf16[1,2688,1024]{2,1,0:T(8,128)(2,1)} %param.9, s32[]{:T(128)S(6)} %select_n.443, s32[]{:T(128)S(6)} %select_n.444), kind=kLoop, calls=%fused_computation.61 | loop fusion | bytes 5505032 | tf_op jit(solution)/shard_map/dynamic_slice | solution.py:230
  18.9 3.5 %collective-permute-start.10 = (bf16[672,256]{1,0:T(8,128)(2,1)}, bf16[672,256]{1,0:T(8,128)(2,1)S(1)}, u32[]{:S(2)}, u32[]{:S(2)}) collective-permute-start(bf16[672,256]{1,0:T(8,128)(2,1)} %fusion.56), channel_id=1, source_target_pairs={{0,16},{16,0},{1,17},{17,1},{2,18},{18,2},{3,19},{19,3},{4,20},{20... | collective-permute-start | bytes 1032200 | tf_op jit(solution)/shard_map/ppermute | solution.py:212
  23.1 7.4 %collective-permute-done.10 = bf16[672,256]{1,0:T(8,128)(2,1)S(1)} collective-permute-done((bf16[672,256]{1,0:T(8,128)(2,1)}, bf16[672,256]{1,0:T(8,128)(2,1)S(1)}, u32[]{:S(2)}, u32[]{:S(2)}) %collective-permute-start.10) | collective-permute-done | bytes 344096 | tf_op jit(solution)/shard_map/ppermute | solution.py:212
  30.7 2.8 collective-permute-start.12
  35.4 5.1 %collective-permute-done = bf16[2688,128]{1,0:T(8,128)(2,1)} collective-permute-done((bf16[2688,128]{1,0:T(8,128)(2,1)S(1)}, bf16[2688,128]{1,0:T(8,128)(2,1)}, u32[]{:S(2)}, u32[]{:S(2)}) %collective-permute-start) | collective-permute-done | bytes 688160 | tf_op jit(solution)/shard_map/ppermute | solution.py:212
  40.5 2.3 collective-permute-start.43
  46.2 16.9 %collective-permute-done.12 = bf16[672,256]{1,0:T(8,128)(2,1)S(1)} collective-permute-done((bf16[672,256]{1,0:T(8,128)(2,1)S(1)}, bf16[672,256]{1,0:T(8,128)(2,1)S(1)}, u32[]{:S(2)}, u32[]{:S(2)}) %collective-permute-start.12) | collective-permute-done | bytes 344096 | tf_op jit(solution)/shard_map/ppermute | solution.py:220
  63.1 2.4 collective-permute-start.44
  67.0 14.7 %collective-permute-start.6 = (bf16[336,1024]{1,0:T(8,128)(2,1)S(1)}, bf16[336,1024]{1,0:T(8,128)(2,1)S(1)}, u32[]{:S(2)}, u32[]{:S(2)}) collective-permute-start(bf16[336,1024]{1,0:T(8,128)(2,1)S(1)} %get-tuple-element.65), channel_id=1, source_target_pairs={{0,4},{4,0},{8,14},{12,10},{18,20},{22,16},{26,30},{30,26},{1,5},{... | collective-permute-start | bytes 2064392 | tf_op jit(solution)/shard_map/ppermute | solution.py:336
  81.8 4.9 %collective-permute-done.43 = bf16[672,256]{1,0:T(8,128)(2,1)S(1)} collective-permute-done((bf16[672,256]{1,0:T(8,128)(2,1)S(1)}, bf16[672,256]{1,0:T(8,128)(2,1)S(1)}, u32[]{:S(2)}, u32[]{:S(2)}) %collective-permute-start.43) | collective-permute-done | bytes 344096 | tf_op jit(solution)/shard_map/ppermute | solution.py:220
  86.7 4.4 %collective-permute-start.5 = (bf16[336,1024]{1,0:T(8,128)(2,1)S(1)}, bf16[336,1024]{1,0:T(8,128)(2,1)S(1)}, u32[]{:S(2)}, u32[]{:S(2)}) collective-permute-start(bf16[336,1024]{1,0:T(8,128)(2,1)S(1)} %get-tuple-element.65), channel_id=1, source_target_pairs={{0,12},{4,8},{8,6},{12,2},{18,28},{22,24},{26,22},{30,18},{1,13},{... | collective-permute-start | bytes 2064392 | tf_op jit(solution)/shard_map/ppermute | solution.py:336
  91.8 5.6 %collective-permute-start.3 = (bf16[336,1024]{1,0:T(8,128)(2,1)S(1)}, bf16[336,1024]{1,0:T(8,128)(2,1)S(1)}, u32[]{:S(2)}, u32[]{:S(2)}) collective-permute-start(bf16[336,1024]{1,0:T(8,128)(2,1)S(1)} %get-tuple-element.65), channel_id=1, source_target_pairs={{0,8},{4,12},{8,2},{12,6},{18,24},{22,28},{26,18},{30,22},{1,9},{5... | collective-permute-start | bytes 2064392 | tf_op jit(solution)/shard_map/ppermute | solution.py:336
  97.7 2.5 collective-permute-done.6
  100.2 11.4 %collective-permute-start.40 = (bf16[336,1024]{1,0:T(8,128)(2,1)S(1)}, bf16[336,1024]{1,0:T(8,128)(2,1)S(1)}, u32[]{:S(2)}, u32[]{:S(2)}) collective-permute-start(bf16[336,1024]{1,0:T(8,128)(2,1)S(1)} %get-tuple-element.64), channel_id=1, source_target_pairs={{0,4},{4,0},{8,14},{12,10},{18,20},{22,16},{26,30},{30,26},{1,5},{... | collective-permute-start | bytes 2064392 | tf_op jit(solution)/shard_map/ppermute | solution.py:336
  127.3 17.8 %collective-permute-start.14 = (bf16[128,256]{1,0:T(8,128)(2,1)S(1)}, bf16[128,256]{1,0:T(8,128)(2,1)S(1)}, u32[]{:S(2)}, u32[]{:S(2)}) collective-permute-start(bf16[128,256]{1,0:T(8,128)(2,1)S(1)} %fusion.120), channel_id=1, source_target_pairs={{0,8},{2,10},{4,12},{6,14},{1,9},{3,11},{5,13},{7,15},{16,24},{18,... | collective-permute-start | bytes 196616 | tf_op jit(solution)/shard_map/ppermute | solution.py:224
  145.1 6.5 %collective-permute-start.15 = (bf16[512,256]{1,0:T(8,128)(2,1)S(1)}, bf16[512,256]{1,0:T(8,128)(2,1)S(1)}, u32[]{:S(2)}, u32[]{:S(2)}) collective-permute-start(bf16[512,256]{1,0:T(8,128)(2,1)S(1)} %pad_maximum_fusion.37.own_ref), channel_id=1, source_target_pairs={{0,4},{2,6},{4,8},{6,10},{8,12},{10,14},{1,5},{3,7},{5,9},{7,11},{... | collective-permute-start | bytes 786440 | tf_op jit(solution)/shard_map/ppermute | solution.py:224
  154.9 3.7 %collective-permute-done.8 = bf16[512,256]{1,0:T(8,128)(2,1)S(1)} collective-permute-done((bf16[512,256]{1,0:T(8,128)(2,1)S(1)}, bf16[512,256]{1,0:T(8,128)(2,1)S(1)}, u32[]{:S(2)}, u32[]{:S(2)}) %collective-permute-start.8) | collective-permute-done | bytes 262176 | tf_op jit(solution)/shard_map/ppermute | solution.py:409
  158.6 4.4 %collective-permute-start.26 = (bf16[512,256]{1,0:T(8,128)(2,1)S(1)}, bf16[512,256]{1,0:T(8,128)(2,1)S(1)}, u32[]{:S(2)}, u32[]{:S(2)}) collective-permute-start(bf16[512,256]{1,0:T(8,128)(2,1)S(1)} %constant_dynamic-slice_fusion.4), channel_id=1, source_target_pairs={{0,16},{1,17},{2,18},{3,19},{4,20},{5,21},{6,22},{7,23},{8,24},{9,... | collective-permute-start | bytes 786440 | tf_op jit(solution)/shard_map/ppermute | solution.py:409
  164.3 2.4 shard_map.73
  168.3 6.0 %collective-permute-done.16 = bf16[512,256]{1,0:T(8,128)(2,1)S(1)} collective-permute-done((bf16[512,256]{1,0:T(8,128)(2,1)S(1)}, bf16[512,256]{1,0:T(8,128)(2,1)S(1)}, u32[]{:S(2)}, u32[]{:S(2)}) %collective-permute-start.16) | collective-permute-done | bytes 262176 | tf_op jit(solution)/shard_map/ppermute | solution.py:212
  177.5 2.4 shard_map.74
  182.1 6.6 %collective-permute-done.29 = bf16[512,256]{1,0:T(8,128)(2,1)S(1)} collective-permute-done((bf16[512,256]{1,0:T(8,128)(2,1)S(1)}, bf16[512,256]{1,0:T(8,128)(2,1)S(1)}, u32[]{:S(2)}, u32[]{:S(2)}) %collective-permute-start.29) | collective-permute-done | bytes 262176 | tf_op jit(solution)/shard_map/ppermute | solution.py:212
  188.7 5.2 %collective-permute-start.37 = (bf16[336,1024]{1,0:T(8,128)(2,1)S(1)}, bf16[336,1024]{1,0:T(8,128)(2,1)S(1)}, u32[]{:S(2)}, u32[]{:S(2)}) collective-permute-start(bf16[336,1024]{1,0:T(8,128)(2,1)S(1)} %get-tuple-element.64), channel_id=1, source_target_pairs={{0,8},{4,12},{8,2},{12,6},{18,24},{22,28},{26,18},{30,22},{1,9},{5... | collective-permute-start | bytes 2064392 | tf_op jit(solution)/shard_map/ppermute | solution.py:336
  198.4 7.6 %collective-permute-done.18 = bf16[672,256]{1,0:T(8,128)(2,1)S(1)} collective-permute-done((bf16[672,256]{1,0:T(8,128)(2,1)S(1)}, bf16[672,256]{1,0:T(8,128)(2,1)S(1)}, u32[]{:S(2)}, u32[]{:S(2)}) %collective-permute-start.18) | collective-permute-done | bytes 344096 | tf_op jit(solution)/shard_map/ppermute | solution.py:212
  207.7 7.6 %collective-permute-done.31 = bf16[672,256]{1,0:T(8,128)(2,1)S(1)} collective-permute-done((bf16[672,256]{1,0:T(8,128)(2,1)S(1)}, bf16[672,256]{1,0:T(8,128)(2,1)S(1)}, u32[]{:S(2)}, u32[]{:S(2)}) %collective-permute-start.31) | collective-permute-done | bytes 344096 | tf_op jit(solution)/shard_map/ppermute | solution.py:212
  217.0 3.8 %collective-permute-done.19 = bf16[672,128]{1,0:T(8,128)(2,1)S(1)} collective-permute-done((bf16[672,128]{1,0:T(8,128)(2,1)S(1)}, bf16[672,128]{1,0:T(8,128)(2,1)S(1)}, u32[]{:S(2)}, u32[]{:S(2)}) %collective-permute-start.19) | collective-permute-done | bytes 172064 | tf_op jit(solution)/shard_map/ppermute | solution.py:212
  228.0 5.4 %collective-permute-done.20 = bf16[672,256]{1,0:T(8,128)(2,1)S(1)} collective-permute-done((bf16[672,256]{1,0:T(8,128)(2,1)S(1)}, bf16[672,256]{1,0:T(8,128)(2,1)S(1)}, u32[]{:S(2)}, u32[]{:S(2)}) %collective-permute-start.20) | collective-permute-done | bytes 344096 | tf_op jit(solution)/shard_map/ppermute | solution.py:212
  233.4 3.7 %collective-permute-done.21 = bf16[672,128]{1,0:T(8,128)(2,1)S(1)} collective-permute-done((bf16[672,128]{1,0:T(8,128)(2,1)S(1)}, bf16[672,128]{1,0:T(8,128)(2,1)S(1)}, u32[]{:S(2)}, u32[]{:S(2)}) %collective-permute-start.21) | collective-permute-done | bytes 172064 | tf_op jit(solution)/shard_map/ppermute | solution.py:212
  237.9 6.3 %collective-permute-done.33 = bf16[672,256]{1,0:T(8,128)(2,1)S(1)} collective-permute-done((bf16[672,256]{1,0:T(8,128)(2,1)S(1)}, bf16[672,256]{1,0:T(8,128)(2,1)S(1)}, u32[]{:S(2)}, u32[]{:S(2)}) %collective-permute-start.33) | collective-permute-done | bytes 344096 | tf_op jit(solution)/shard_map/ppermute | solution.py:212
  246.6 5.4 %collective-permute-done.35 = bf16[672,256]{1,0:T(8,128)(2,1)S(1)} collective-permute-done((bf16[672,256]{1,0:T(8,128)(2,1)S(1)}, bf16[672,256]{1,0:T(8,128)(2,1)S(1)}, u32[]{:S(2)}, u32[]{:S(2)}) %collective-permute-start.35) | collective-permute-done | bytes 344096 | tf_op jit(solution)/shard_map/ppermute | solution.py:212
  259.8 2.0 fusion.127
  263.7 1.9 collective-permute-start.45
  267.0 2.3 collective-permute-start.46
  271.5 5.2 %collective-permute-done.41 = bf16[512,256]{1,0:T(8,128)(2,1)S(1)} collective-permute-done((bf16[512,256]{1,0:T(8,128)(2,1)S(1)}, bf16[512,256]{1,0:T(8,128)(2,1)S(1)}, u32[]{:S(2)}, u32[]{:S(2)}) %collective-permute-start.41) | collective-permute-done | bytes 262176 | tf_op jit(solution)/shard_map/ppermute | solution.py:409
  276.8 2.4 shard_map.75
  280.0 4.1 %collective-permute-start.53 = (bf16[128,256]{1,0:T(8,128)(2,1)S(1)}, bf16[128,256]{1,0:T(8,128)(2,1)S(1)}, u32[]{:S(2)}, u32[]{:S(2)}) collective-permute-start(bf16[128,256]{1,0:T(8,128)(2,1)S(1)} %fusion.117), channel_id=1, source_target_pairs={{0,8},{2,10},{4,12},{6,14},{1,9},{3,11},{5,13},{7,15},{16,24},{18,... | collective-permute-start | bytes 196616 | tf_op jit(solution)/shard_map/ppermute | solution.py:224
  284.1 1.9 collective-permute-start.54
  287.8 3.5 %collective-permute-done.54.near_ref = bf16[512,256]{1,0:T(8,128)(2,1)S(1)} collective-permute-done((bf16[512,256]{1,0:T(8,128)(2,1)S(1)}, bf16[512,256]{1,0:T(8,128)(2,1)S(1)}, u32[]{:S(2)}, u32[]{:S(2)}) %collective-permute-start.54) | collective-permute-done | bytes 262176 | tf_op jit(solution)/shard_map/ppermute | solution.py:224
  291.2 2.4 shard_map.76
  294.1 6.4 %collective-permute-done.55 = bf16[512,256]{1,0:T(8,128)(2,1)S(1)} collective-permute-done((bf16[512,256]{1,0:T(8,128)(2,1)S(1)}, bf16[512,256]{1,0:T(8,128)(2,1)S(1)}, u32[]{:S(2)}, u32[]{:S(2)}) %collective-permute-start.55) | collective-permute-done | bytes 262176 | tf_op jit(solution)/shard_map/ppermute | solution.py:212
  304.8 7.7 %collective-permute-done.49 = bf16[672,256]{1,0:T(8,128)(2,1)S(1)} collective-permute-done((bf16[672,256]{1,0:T(8,128)(2,1)S(1)}, bf16[672,256]{1,0:T(8,128)(2,1)S(1)}, u32[]{:S(2)}, u32[]{:S(2)}) %collective-permute-start.49) | collective-permute-done | bytes 344096 | tf_op jit(solution)/shard_map/ppermute | solution.py:212
  312.7 2.7 collective-permute-start.50
  317.0 2.6 collective-permute-done.57
  319.7 2.5 collective-permute-start.58
  322.5 6.8 %collective-permute-done.58 = bf16[672,256]{1,0:T(8,128)(2,1)S(1)} collective-permute-done((bf16[672,256]{1,0:T(8,128)(2,1)S(1)}, bf16[672,256]{1,0:T(8,128)(2,1)S(1)}, u32[]{:S(2)}, u32[]{:S(2)}) %collective-permute-start.58) | collective-permute-done | bytes 344096 | tf_op jit(solution)/shard_map/ppermute | solution.py:462
  (259 shorter events, 87.1 us)
Async XLA Ops:
  1.3 21.1 %collective-permute-start.7 = (bf16[2688]{0:T(1024)(128)(2,1)}, bf16[2688]{0:T(1024)(128)(2,1)}, u32[]{:S(2)}, u32[]{:S(2)}) collective-permute-start(bf16[2688]{0:T(1024)(128)(2,1)} %reduce), channel_id=1, source_target_pairs={{0,16},{16,0},{1,17},{17,1},{2,18},{18,2},{3,19},{19,3},{4,20},{20... | collective-permute-start | bytes 16136 | tf_op jit(solution)/shard_map/ppermute | solution.py:212
  6.4 11.5 %collective-permute-start.9 = (bf16[336,512]{1,0:T(8,128)(2,1)S(1)}, bf16[336,512]{1,0:T(8,128)(2,1)S(1)}, u32[]{:S(2)}, u32[]{:S(2)}) collective-permute-start(bf16[336,512]{1,0:T(8,128)(2,1)S(1)} %pad_maximum_fusion.30), channel_id=1, source_target_pairs={{0,2},{2,0},{4,6},{6,4},{8,10},{10,8},{12,14},{14,12},{1,3},{3,1},... | collective-permute-start | bytes 1032200 | tf_op jit(solution)/shard_map/ppermute | solution.py:216
  6.5 38.1 %collective-permute-start.2 = (bf16[336,1024]{1,0:T(8,128)(2,1)}, bf16[336,1024]{1,0:T(8,128)(2,1)}, u32[]{:S(2)}, u32[]{:S(2)}) collective-permute-start(bf16[336,1024]{1,0:T(8,128)(2,1)} %bitcast.4), channel_id=1, source_target_pairs={{2,18},{6,22},{10,26},{14,30},{16,0},{20,4},{24,8},{28,12},{3,19},... | collective-permute-start | bytes 2064392 | tf_op jit(solution)/shard_map/ppermute | solution.py:320
  8.2 27.1 %collective-permute-start.24 = (bf16[2688,128]{1,0:T(8,128)(2,1)S(1)}, bf16[2688,128]{1,0:T(8,128)(2,1)}, u32[]{:S(2)}, u32[]{:S(2)}) collective-permute-start(bf16[2688,128]{1,0:T(8,128)(2,1)S(1)} %bitcast.80), channel_id=1, source_target_pairs={{0,1},{1,0},{2,3},{3,2},{4,5},{5,4},{6,7},{7,6},{8,9},{9,8},{10,11... | collective-permute-start | bytes 2064392 | tf_op jit(solution)/shard_map/ppermute | solution.py:212
  10.2 30.3 %collective-permute-start = (bf16[2688,128]{1,0:T(8,128)(2,1)S(1)}, bf16[2688,128]{1,0:T(8,128)(2,1)}, u32[]{:S(2)}, u32[]{:S(2)}) collective-permute-start(bf16[2688,128]{1,0:T(8,128)(2,1)S(1)} %bitcast.81), channel_id=1, source_target_pairs={{0,1},{1,0},{2,3},{3,2},{4,5},{5,4},{6,7},{7,6},{8,9},{9,8},{10,11... | collective-permute-start | bytes 2064392 | tf_op jit(solution)/shard_map/ppermute | solution.py:212
  18.9 11.6 %collective-permute-start.10 = (bf16[672,256]{1,0:T(8,128)(2,1)}, bf16[672,256]{1,0:T(8,128)(2,1)S(1)}, u32[]{:S(2)}, u32[]{:S(2)}) collective-permute-start(bf16[672,256]{1,0:T(8,128)(2,1)} %fusion.56), channel_id=1, source_target_pairs={{0,16},{16,0},{1,17},{17,1},{2,18},{18,2},{3,19},{19,3},{4,20},{20... | collective-permute-start | bytes 1032200 | tf_op jit(solution)/shard_map/ppermute | solution.py:212
  30.7 32.4 %collective-permute-start.12 = (bf16[672,256]{1,0:T(8,128)(2,1)S(1)}, bf16[672,256]{1,0:T(8,128)(2,1)S(1)}, u32[]{:S(2)}, u32[]{:S(2)}) collective-permute-start(bf16[672,256]{1,0:T(8,128)(2,1)S(1)} %get-tuple-element.16), channel_id=1, source_target_pairs={{0,8},{2,10},{4,12},{6,14},{8,0},{10,2},{12,4},{14,6},{1,9},{3,11}... | collective-permute-start | bytes 1032200 | tf_op jit(solution)/shard_map/ppermute | solution.py:220
  33.5 31.9 %collective-permute-start.11 = (bf16[672,256]{1,0:T(8,128)(2,1)S(1)}, bf16[672,256]{1,0:T(8,128)(2,1)S(1)}, u32[]{:S(2)}, u32[]{:S(2)}) collective-permute-start(bf16[672,256]{1,0:T(8,128)(2,1)S(1)} %get-tuple-element.16), channel_id=1, source_target_pairs={{0,4},{2,6},{4,0},{6,2},{8,12},{10,14},{12,8},{14,10},{1,5},{3,7},... | collective-permute-start | bytes 1032200 | tf_op jit(solution)/shard_map/ppermute | solution.py:220
  35.3 31.7 %collective-permute-start.13 = (bf16[672,256]{1,0:T(8,128)(2,1)S(1)}, bf16[672,256]{1,0:T(8,128)(2,1)S(1)}, u32[]{:S(2)}, u32[]{:S(2)}) collective-permute-start(bf16[672,256]{1,0:T(8,128)(2,1)S(1)} %get-tuple-element.16), channel_id=1, source_target_pairs={{0,12},{2,14},{4,8},{6,10},{8,4},{10,6},{12,0},{14,2},{1,13},{3,15... | collective-permute-start | bytes 1032200 | tf_op jit(solution)/shard_map/ppermute | solution.py:220
  40.5 46.2 %collective-permute-start.43 = (bf16[672,256]{1,0:T(8,128)(2,1)S(1)}, bf16[672,256]{1,0:T(8,128)(2,1)S(1)}, u32[]{:S(2)}, u32[]{:S(2)}) collective-permute-start(bf16[672,256]{1,0:T(8,128)(2,1)S(1)} %get-tuple-element.6), channel_id=1, source_target_pairs={{0,8},{2,10},{4,12},{6,14},{8,0},{10,2},{12,4},{14,6},{1,9},{3,11}... | collective-permute-start | bytes 1032200 | tf_op jit(solution)/shard_map/ppermute | solution.py:220
  44.6 46.5 %collective-permute-start.42 = (bf16[672,256]{1,0:T(8,128)(2,1)S(1)}, bf16[672,256]{1,0:T(8,128)(2,1)S(1)}, u32[]{:S(2)}, u32[]{:S(2)}) collective-permute-start(bf16[672,256]{1,0:T(8,128)(2,1)S(1)} %get-tuple-element.6), channel_id=1, source_target_pairs={{0,4},{2,6},{4,0},{6,2},{8,12},{10,14},{12,8},{14,10},{1,5},{3,7},... | collective-permute-start | bytes 1032200 | tf_op jit(solution)/shard_map/ppermute | solution.py:220
  63.1 28.7 %collective-permute-start.44 = (bf16[672,256]{1,0:T(8,128)(2,1)S(1)}, bf16[672,256]{1,0:T(8,128)(2,1)S(1)}, u32[]{:S(2)}, u32[]{:S(2)}) collective-permute-start(bf16[672,256]{1,0:T(8,128)(2,1)S(1)} %get-tuple-element.6), channel_id=1, source_target_pairs={{0,12},{2,14},{4,8},{6,10},{8,4},{10,6},{12,0},{14,2},{1,13},{3,15... | collective-permute-start | bytes 1032200 | tf_op jit(solution)/shard_map/ppermute | solution.py:220
  65.5 48.1 %collective-permute-start.1 = (bf16[2688,256]{1,0:T(8,128)(2,1)S(1)}, bf16[2688,256]{1,0:T(8,128)(2,1)S(1)}, u32[]{:S(2)}, u32[]{:S(2)}) collective-permute-start(bf16[2688,256]{1,0:T(8,128)(2,1)S(1)} %pad_maximum_fusion.5), channel_id=1, source_target_pairs={{0,2},{2,0},{4,6},{6,4},{8,10},{10,8},{12,14},{14,12},{1,3},{3,1},... | collective-permute-start | bytes 4128776 | tf_op jit(solution)/shard_map/ppermute | solution.py:216
  67.0 33.2 %collective-permute-start.6 = (bf16[336,1024]{1,0:T(8,128)(2,1)S(1)}, bf16[336,1024]{1,0:T(8,128)(2,1)S(1)}, u32[]{:S(2)}, u32[]{:S(2)}) collective-permute-start(bf16[336,1024]{1,0:T(8,128)(2,1)S(1)} %get-tuple-element.65), channel_id=1, source_target_pairs={{0,4},{4,0},{8,14},{12,10},{18,20},{22,16},{26,30},{30,26},{1,5},{... | collective-permute-start | bytes 2064392 | tf_op jit(solution)/shard_map/ppermute | solution.py:336
  86.7 25.0 %collective-permute-start.5 = (bf16[336,1024]{1,0:T(8,128)(2,1)S(1)}, bf16[336,1024]{1,0:T(8,128)(2,1)S(1)}, u32[]{:S(2)}, u32[]{:S(2)}) collective-permute-start(bf16[336,1024]{1,0:T(8,128)(2,1)S(1)} %get-tuple-element.65), channel_id=1, source_target_pairs={{0,12},{4,8},{8,6},{12,2},{18,28},{22,24},{26,22},{30,18},{1,13},{... | collective-permute-start | bytes 2064392 | tf_op jit(solution)/shard_map/ppermute | solution.py:336
  91.1 22.1 %collective-permute-start.4 = (bf16[336,1024]{1,0:T(8,128)(2,1)S(1)}, bf16[336,1024]{1,0:T(8,128)(2,1)S(1)}, u32[]{:S(2)}, u32[]{:S(2)}) collective-permute-start(bf16[336,1024]{1,0:T(8,128)(2,1)S(1)} %get-tuple-element.65), channel_id=1, source_target_pairs={{0,0},{4,4},{8,10},{12,14},{18,16},{22,20},{26,26},{30,30},{1,1},{... | collective-permute-start | bytes 2064392 | tf_op jit(solution)/shard_map/ppermute | solution.py:336
  91.8 21.5 %collective-permute-start.3 = (bf16[336,1024]{1,0:T(8,128)(2,1)S(1)}, bf16[336,1024]{1,0:T(8,128)(2,1)S(1)}, u32[]{:S(2)}, u32[]{:S(2)}) collective-permute-start(bf16[336,1024]{1,0:T(8,128)(2,1)S(1)} %get-tuple-element.65), channel_id=1, source_target_pairs={{0,8},{4,12},{8,2},{12,6},{18,24},{22,28},{26,18},{30,22},{1,9},{5... | collective-permute-start | bytes 2064392 | tf_op jit(solution)/shard_map/ppermute | solution.py:336
  100.2 122.1 %collective-permute-start.40 = (bf16[336,1024]{1,0:T(8,128)(2,1)S(1)}, bf16[336,1024]{1,0:T(8,128)(2,1)S(1)}, u32[]{:S(2)}, u32[]{:S(2)}) collective-permute-start(bf16[336,1024]{1,0:T(8,128)(2,1)S(1)} %get-tuple-element.64), channel_id=1, source_target_pairs={{0,4},{4,0},{8,14},{12,10},{18,20},{22,16},{26,30},{30,26},{1,5},{... | collective-permute-start | bytes 2064392 | tf_op jit(solution)/shard_map/ppermute | solution.py:336
  111.6 112.4 %collective-permute-start.39 = (bf16[336,1024]{1,0:T(8,128)(2,1)S(1)}, bf16[336,1024]{1,0:T(8,128)(2,1)S(1)}, u32[]{:S(2)}, u32[]{:S(2)}) collective-permute-start(bf16[336,1024]{1,0:T(8,128)(2,1)S(1)} %get-tuple-element.64), channel_id=1, source_target_pairs={{0,12},{4,8},{8,6},{12,2},{18,28},{22,24},{26,22},{30,18},{1,13},{... | collective-permute-start | bytes 2064392 | tf_op jit(solution)/shard_map/ppermute | solution.py:336
  127.3 35.8 %collective-permute-start.14 = (bf16[128,256]{1,0:T(8,128)(2,1)S(1)}, bf16[128,256]{1,0:T(8,128)(2,1)S(1)}, u32[]{:S(2)}, u32[]{:S(2)}) collective-permute-start(bf16[128,256]{1,0:T(8,128)(2,1)S(1)} %fusion.120), channel_id=1, source_target_pairs={{0,8},{2,10},{4,12},{6,14},{1,9},{3,11},{5,13},{7,15},{16,24},{18,... | collective-permute-start | bytes 196616 | tf_op jit(solution)/shard_map/ppermute | solution.py:224
  145.1 19.2 %collective-permute-start.15 = (bf16[512,256]{1,0:T(8,128)(2,1)S(1)}, bf16[512,256]{1,0:T(8,128)(2,1)S(1)}, u32[]{:S(2)}, u32[]{:S(2)}) collective-permute-start(bf16[512,256]{1,0:T(8,128)(2,1)S(1)} %pad_maximum_fusion.37.own_ref), channel_id=1, source_target_pairs={{0,4},{2,6},{4,8},{6,10},{8,12},{10,14},{1,5},{3,7},{5,9},{7,11},{... | collective-permute-start | bytes 786440 | tf_op jit(solution)/shard_map/ppermute | solution.py:224
  158.6 8.3 %collective-permute-start.26 = (bf16[512,256]{1,0:T(8,128)(2,1)S(1)}, bf16[512,256]{1,0:T(8,128)(2,1)S(1)}, u32[]{:S(2)}, u32[]{:S(2)}) collective-permute-start(bf16[512,256]{1,0:T(8,128)(2,1)S(1)} %constant_dynamic-slice_fusion.4), channel_id=1, source_target_pairs={{0,16},{1,17},{2,18},{3,19},{4,20},{5,21},{6,22},{7,23},{8,24},{9,... | collective-permute-start | bytes 786440 | tf_op jit(solution)/shard_map/ppermute | solution.py:409
  163.1 60.9 %collective-permute-start.38 = (bf16[336,1024]{1,0:T(8,128)(2,1)S(1)}, bf16[336,1024]{1,0:T(8,128)(2,1)S(1)}, u32[]{:S(2)}, u32[]{:S(2)}) collective-permute-start(bf16[336,1024]{1,0:T(8,128)(2,1)S(1)} %get-tuple-element.64), channel_id=1, source_target_pairs={{0,0},{4,4},{8,10},{12,14},{18,16},{22,20},{26,26},{30,30},{1,1},{... | collective-permute-start | bytes 2064392 | tf_op jit(solution)/shard_map/ppermute | solution.py:336
  166.7 7.7 %collective-permute-start.16 = (bf16[512,256]{1,0:T(8,128)(2,1)S(1)}, bf16[512,256]{1,0:T(8,128)(2,1)S(1)}, u32[]{:S(2)}, u32[]{:S(2)}) collective-permute-start(bf16[512,256]{1,0:T(8,128)(2,1)S(1)} %shard_map.73), channel_id=1, source_target_pairs={{0,16},{16,0},{1,17},{17,1},{2,18},{18,2},{3,19},{19,3},{4,20},{20... | collective-permute-start | bytes 786440 | tf_op jit(solution)/shard_map/ppermute | solution.py:212
  166.9 10.6 %collective-permute-start.28 = (bf16[512,256]{1,0:T(8,128)(2,1)S(1)}, bf16[512,256]{1,0:T(8,128)(2,1)S(1)}, u32[]{:S(2)}, u32[]{:S(2)}) collective-permute-start(bf16[512,256]{1,0:T(8,128)(2,1)S(1)} %pad_maximum_fusion.38.own_ref), channel_id=1, source_target_pairs={{0,4},{2,6},{4,8},{6,10},{8,12},{10,14},{1,5},{3,7},{5,9},{7,11},{... | collective-permute-start | bytes 786440 | tf_op jit(solution)/shard_map/ppermute | solution.py:224
  177.5 16.4 %collective-permute-start.17 = (bf16[512,512]{1,0:T(8,128)(2,1)S(1)}, bf16[512,512]{1,0:T(8,128)(2,1)S(1)}, u32[]{:S(2)}, u32[]{:S(2)}) collective-permute-start(bf16[512,512]{1,0:T(8,128)(2,1)S(1)} %pad_maximum_fusion.18), channel_id=1, source_target_pairs={{0,2},{2,0},{4,6},{6,4},{8,10},{10,8},{12,14},{14,12},{1,3},{3,1},... | collective-permute-start | bytes 1572872 | tf_op jit(solution)/shard_map/ppermute | solution.py:216
  179.9 8.8 %collective-permute-start.29 = (bf16[512,256]{1,0:T(8,128)(2,1)S(1)}, bf16[512,256]{1,0:T(8,128)(2,1)S(1)}, u32[]{:S(2)}, u32[]{:S(2)}) collective-permute-start(bf16[512,256]{1,0:T(8,128)(2,1)S(1)} %shard_map.74), channel_id=1, source_target_pairs={{0,16},{16,0},{1,17},{17,1},{2,18},{18,2},{3,19},{19,3},{4,20},{20... | collective-permute-start | bytes 786440 | tf_op jit(solution)/shard_map/ppermute | solution.py:212
  188.7 35.4 %collective-permute-start.37 = (bf16[336,1024]{1,0:T(8,128)(2,1)S(1)}, bf16[336,1024]{1,0:T(8,128)(2,1)S(1)}, u32[]{:S(2)}, u32[]{:S(2)}) collective-permute-start(bf16[336,1024]{1,0:T(8,128)(2,1)S(1)} %get-tuple-element.64), channel_id=1, source_target_pairs={{0,8},{4,12},{8,2},{12,6},{18,24},{22,28},{26,18},{30,22},{1,9},{5... | collective-permute-start | bytes 2064392 | tf_op jit(solution)/shard_map/ppermute | solution.py:336
  195.9 10.1 %collective-permute-start.18 = (bf16[672,256]{1,0:T(8,128)(2,1)S(1)}, bf16[672,256]{1,0:T(8,128)(2,1)S(1)}, u32[]{:S(2)}, u32[]{:S(2)}) collective-permute-start(bf16[672,256]{1,0:T(8,128)(2,1)S(1)} %dynamic-slice_convert_fusion.3), channel_id=1, source_target_pairs={{0,1},{1,0},{2,3},{3,2},{4,5},{5,4},{6,7},{7,6},{8,9},{9,8},{10,11... | collective-permute-start | bytes 1032200 | tf_op jit(solution)/shard_map/ppermute | solution.py:212
  206.0 9.3 %collective-permute-start.31 = (bf16[672,256]{1,0:T(8,128)(2,1)S(1)}, bf16[672,256]{1,0:T(8,128)(2,1)S(1)}, u32[]{:S(2)}, u32[]{:S(2)}) collective-permute-start(bf16[672,256]{1,0:T(8,128)(2,1)S(1)} %dynamic-slice_convert_fusion.2), channel_id=1, source_target_pairs={{0,1},{1,0},{2,3},{3,2},{4,5},{5,4},{6,7},{7,6},{8,9},{9,8},{10,11... | collective-permute-start | bytes 1032200 | tf_op jit(solution)/shard_map/ppermute | solution.py:212
  222.3 11.1 %collective-permute-start.20 = (bf16[672,256]{1,0:T(8,128)(2,1)S(1)}, bf16[672,256]{1,0:T(8,128)(2,1)S(1)}, u32[]{:S(2)}, u32[]{:S(2)}) collective-permute-start(bf16[672,256]{1,0:T(8,128)(2,1)S(1)} %pad_maximum_fusion.31), channel_id=1, source_target_pairs={{0,16},{16,0},{1,17},{17,1},{2,18},{18,2},{3,19},{19,3},{4,20},{20... | collective-permute-start | bytes 1032200 | tf_op jit(solution)/shard_map/ppermute | solution.py:212
  224.4 12.7 %collective-permute-start.21 = (bf16[672,128]{1,0:T(8,128)(2,1)S(1)}, bf16[672,128]{1,0:T(8,128)(2,1)S(1)}, u32[]{:S(2)}, u32[]{:S(2)}) collective-permute-start(bf16[672,128]{1,0:T(8,128)(2,1)S(1)} %get-tuple-element.177), channel_id=1, source_target_pairs={{0,16},{16,0},{1,17},{17,1},{2,18},{18,2},{3,19},{19,3},{4,20},{20... | collective-permute-start | bytes 516104 | tf_op jit(solution)/shard_map/ppermute | solution.py:212
  224.9 19.4 %collective-permute-start.34 = (bf16[672,128]{1,0:T(8,128)(2,1)S(1)}, bf16[672,128]{1,0:T(8,128)(2,1)S(1)}, u32[]{:S(2)}, u32[]{:S(2)}) collective-permute-start(bf16[672,128]{1,0:T(8,128)(2,1)S(1)} %get-tuple-element.191), channel_id=1, source_target_pairs={{0,16},{16,0},{1,17},{17,1},{2,18},{18,2},{3,19},{19,3},{4,20},{20... | collective-permute-start | bytes 516104 | tf_op jit(solution)/shard_map/ppermute | solution.py:212
  226.6 17.7 %collective-permute-start.33 = (bf16[672,256]{1,0:T(8,128)(2,1)S(1)}, bf16[672,256]{1,0:T(8,128)(2,1)S(1)}, u32[]{:S(2)}, u32[]{:S(2)}) collective-permute-start(bf16[672,256]{1,0:T(8,128)(2,1)S(1)} %pad_maximum_fusion.34), channel_id=1, source_target_pairs={{0,16},{16,0},{1,17},{17,1},{2,18},{18,2},{3,19},{19,3},{4,20},{20... | collective-permute-start | bytes 1032200 | tf_op jit(solution)/shard_map/ppermute | solution.py:212
  237.3 8.5 %collective-permute-start.22 = (bf16[672,256]{1,0:T(8,128)(2,1)S(1)}, bf16[672,256]{1,0:T(8,128)(2,1)S(1)}, u32[]{:S(2)}, u32[]{:S(2)}) collective-permute-start(bf16[672,256]{1,0:T(8,128)(2,1)S(1)} %get-tuple-element.200), channel_id=1, source_target_pairs={{0,1},{1,0},{2,3},{3,2},{4,5},{5,4},{6,7},{7,6},{8,9},{9,8},{10,11... | collective-permute-start | bytes 1032200 | tf_op jit(solution)/shard_map/ppermute | solution.py:212
  244.5 7.5 %collective-permute-start.35 = (bf16[672,256]{1,0:T(8,128)(2,1)S(1)}, bf16[672,256]{1,0:T(8,128)(2,1)S(1)}, u32[]{:S(2)}, u32[]{:S(2)}) collective-permute-start(bf16[672,256]{1,0:T(8,128)(2,1)S(1)} %get-tuple-element.201), channel_id=1, source_target_pairs={{0,1},{1,0},{2,3},{3,2},{4,5},{5,4},{6,7},{7,6},{8,9},{9,8},{10,11... | collective-permute-start | bytes 1032200 | tf_op jit(solution)/shard_map/ppermute | solution.py:212
  263.7 13.1 %collective-permute-start.45 = (bf16[128,256]{1,0:T(8,128)(2,1)S(1)}, bf16[128,256]{1,0:T(8,128)(2,1)S(1)}, u32[]{:S(2)}, u32[]{:S(2)}) collective-permute-start(bf16[128,256]{1,0:T(8,128)(2,1)S(1)} %fusion.118), channel_id=1, source_target_pairs={{0,8},{2,10},{4,12},{6,14},{1,9},{3,11},{5,13},{7,15},{16,24},{18,... | collective-permute-start | bytes 196616 | tf_op jit(solution)/shard_map/ppermute | solution.py:224
  265.7 11.0 %collective-permute-start.41 = (bf16[512,256]{1,0:T(8,128)(2,1)S(1)}, bf16[512,256]{1,0:T(8,128)(2,1)S(1)}, u32[]{:S(2)}, u32[]{:S(2)}) collective-permute-start(bf16[512,256]{1,0:T(8,128)(2,1)S(1)} %constant_dynamic-slice_fusion.3), channel_id=1, source_target_pairs={{16,0},{17,1},{18,2},{19,3},{20,4},{21,5},{22,6},{23,7},{24,8},{25... | collective-permute-start | bytes 786440 | tf_op jit(solution)/shard_map/ppermute | solution.py:409
  267.0 9.8 %collective-permute-start.46 = (bf16[512,256]{1,0:T(8,128)(2,1)S(1)}, bf16[512,256]{1,0:T(8,128)(2,1)S(1)}, u32[]{:S(2)}, u32[]{:S(2)}) collective-permute-start(bf16[512,256]{1,0:T(8,128)(2,1)S(1)} %pad_maximum_fusion.39.own_ref), channel_id=1, source_target_pairs={{0,4},{2,6},{4,8},{6,10},{8,12},{10,14},{1,5},{3,7},{5,9},{7,11},{... | collective-permute-start | bytes 786440 | tf_op jit(solution)/shard_map/ppermute | solution.py:224
  270.2 17.5 %collective-permute-start.52 = (bf16[512,256]{1,0:T(8,128)(2,1)S(1)}, bf16[512,256]{1,0:T(8,128)(2,1)S(1)}, u32[]{:S(2)}, u32[]{:S(2)}) collective-permute-start(bf16[512,256]{1,0:T(8,128)(2,1)S(1)} %constant_dynamic-slice_fusion.1), channel_id=1, source_target_pairs={{16,0},{17,1},{18,2},{19,3},{20,4},{21,5},{22,6},{23,7},{24,8},{25... | collective-permute-start | bytes 786440 | tf_op jit(solution)/shard_map/ppermute | solution.py:409
  279.2 8.4 %collective-permute-start.47 = (bf16[512,256]{1,0:T(8,128)(2,1)S(1)}, bf16[512,256]{1,0:T(8,128)(2,1)S(1)}, u32[]{:S(2)}, u32[]{:S(2)}) collective-permute-start(bf16[512,256]{1,0:T(8,128)(2,1)S(1)} %shard_map.75), channel_id=1, source_target_pairs={{0,16},{16,0},{1,17},{17,1},{2,18},{18,2},{3,19},{19,3},{4,20},{20... | collective-permute-start | bytes 786440 | tf_op jit(solution)/shard_map/ppermute | solution.py:212
  280.0 7.7 %collective-permute-start.53 = (bf16[128,256]{1,0:T(8,128)(2,1)S(1)}, bf16[128,256]{1,0:T(8,128)(2,1)S(1)}, u32[]{:S(2)}, u32[]{:S(2)}) collective-permute-start(bf16[128,256]{1,0:T(8,128)(2,1)S(1)} %fusion.117), channel_id=1, source_target_pairs={{0,8},{2,10},{4,12},{6,14},{1,9},{3,11},{5,13},{7,15},{16,24},{18,... | collective-permute-start | bytes 196616 | tf_op jit(solution)/shard_map/ppermute | solution.py:224
  287.6 13.0 %collective-permute-start.48 = (bf16[512,512]{1,0:T(8,128)(2,1)S(1)}, bf16[512,512]{1,0:T(8,128)(2,1)S(1)}, u32[]{:S(2)}, u32[]{:S(2)}) collective-permute-start(bf16[512,512]{1,0:T(8,128)(2,1)S(1)} %pad_maximum_fusion.22), channel_id=1, source_target_pairs={{0,2},{2,0},{4,6},{6,4},{8,10},{10,8},{12,14},{14,12},{1,3},{3,1},... | collective-permute-start | bytes 1572872 | tf_op jit(solution)/shard_map/ppermute | solution.py:216
  301.6 10.9 %collective-permute-start.49 = (bf16[672,256]{1,0:T(8,128)(2,1)S(1)}, bf16[672,256]{1,0:T(8,128)(2,1)S(1)}, u32[]{:S(2)}, u32[]{:S(2)}) collective-permute-start(bf16[672,256]{1,0:T(8,128)(2,1)S(1)} %dynamic-slice_convert_fusion.1), channel_id=1, source_target_pairs={{0,1},{1,0},{2,3},{3,2},{4,5},{5,4},{6,7},{7,6},{8,9},{9,8},{10,11... | collective-permute-start | bytes 1032200 | tf_op jit(solution)/shard_map/ppermute | solution.py:212
  303.5 16.0 %collective-permute-start.57 = (bf16[672,256]{1,0:T(8,128)(2,1)S(1)}, bf16[672,256]{1,0:T(8,128)(2,1)S(1)}, u32[]{:S(2)}, u32[]{:S(2)}) collective-permute-start(bf16[672,256]{1,0:T(8,128)(2,1)S(1)} %dynamic-slice_convert_fusion), channel_id=1, source_target_pairs={{0,1},{1,0},{2,3},{3,2},{4,5},{5,4},{6,7},{7,6},{8,9},{9,8},{10,11... | collective-permute-start | bytes 1032200 | tf_op jit(solution)/shard_map/ppermute | solution.py:212
  312.7 9.5 %collective-permute-start.50 = (bf16[672,256]{1,0:T(8,128)(2,1)S(1)}, bf16[672,256]{1,0:T(8,128)(2,1)S(1)}, u32[]{:S(2)}, u32[]{:S(2)}) collective-permute-start(bf16[672,256]{1,0:T(8,128)(2,1)S(1)} %add_convert_fusion.1), channel_id=1, source_target_pairs={{0,16},{1,17},{2,18},{3,19},{4,20},{5,21},{6,22},{7,23},{8,24},{9,... | collective-permute-start | bytes 1032200 | tf_op jit(solution)/shard_map/ppermute | solution.py:462
  319.7 9.7 %collective-permute-start.58 = (bf16[672,256]{1,0:T(8,128)(2,1)S(1)}, bf16[672,256]{1,0:T(8,128)(2,1)S(1)}, u32[]{:S(2)}, u32[]{:S(2)}) collective-permute-start(bf16[672,256]{1,0:T(8,128)(2,1)S(1)} %add_convert_fusion), channel_id=1, source_target_pairs={{0,16},{1,17},{2,18},{3,19},{4,20},{5,21},{6,22},{7,23},{8,24},{9,... | collective-permute-start | bytes 1032200 | tf_op jit(solution)/shard_map/ppermute | solution.py:462
  322.4 7.2 %collective-permute-start.51 = (bf16[1344,128]{1,0:T(8,128)(2,1)S(1)}, bf16[1344,128]{1,0:T(8,128)(2,1)S(1)}, u32[]{:S(2)}, u32[]{:S(2)}) collective-permute-start(bf16[1344,128]{1,0:T(8,128)(2,1)S(1)} %constant_dynamic-slice_fusion.2), channel_id=1, source_target_pairs={{0,2},{2,0},{4,6},{6,4},{8,10},{10,8},{12,14},{14,12},{1,3},{3,1},... | collective-permute-start | bytes 1032200 | tf_op jit(solution)/shard_map/ppermute | solution.py:216
  (20 other events, 77.4 us)
